TPU v7x, 512 devices: a whole 4x8x8 slice. The times are simulated.
512 devices in a mesh: scan: 128 (over z, y, core), mode: 4 (over x).
Axes of the slice: x: 4, y: 8, z: 8, core: 2. Of those that a mesh axis runs over, the one named last changes fastest.
Arguments:
- object_tiles: float32 [128, 2, 256, 256], P('scan'), may hold values from -6 to 6
- probe: float32 [4, 2, 256, 256], P('mode'), may hold values from -4 to 4
- measured: float32 [128, 256, 256], P('scan'), may hold values from 0.5 to 4
- cover: int32 [128], P('scan'), may hold values from 0 to 127, as said below
- counts: int32 [128], P('scan'), may hold values from 1 to 1, as said below
- phase: float32 [256, 256], replicated, may hold values from -3.140625 to 3.140625
Outputs:
- object_grad: float32 [128, 2, 256, 256], P('scan')
- probe_grad: float32 [4, 2, 256, 256], P('mode')
- loss: float32 [], replicated
Inputs may be any that keep to these rules, and one draw needn't show every extreme that they name: The slots of group g cover tiles g - 2 to g + 2 only, within the object. `counts`: every group's single slot is live.
All inputs are finite; a program needn't handle non-finite values.
Results may differ from a plain program's by a relative error of at most 0.00019.
Values sent between devices are 32-bit elements; how exact they have to be, the bound alone decides.
No kernel may reach another device: no remote copies, remote signals or barrier semaphores. Data moves between devices by JAX's collectives and lax.ppermute only.
A program may use at most 64 MiB of HBM per device.

v0:
```python
import math

import jax
import jax.numpy as jnp
from jax import lax
from jax.sharding import PartitionSpec as P

REACH = 2


def passed_along(block, axis, distance):
    devices = range(lax.axis_size(axis))
    route = [(i - distance, i) for i in devices if i - distance in devices]
    return lax.ppermute(block, axis, route)


def dft_tables(width_px):
    indices = jnp.arange(width_px, dtype=jnp.int32)
    product = indices[:, None] * indices[None, :] % width_px
    angles = product.astype(jnp.float32) * (2.0 * math.pi / width_px)
    return (jnp.cos(angles), jnp.sin(angles))


def from_left(matrix, field):
    return jnp.einsum("ij,...jk->...ik", matrix, field, precision=lax.Precision.HIGHEST)


def from_right(field, matrix):
    return jnp.einsum("...jk,kl->...jl", field, matrix, precision=lax.Precision.HIGHEST)


def transform(real_part, imag_part, tables, direction_sign):
    cosine_table, sine_table = tables
    signed_sine = direction_sign * sine_table
    mid_real = from_left(cosine_table, real_part) - from_left(signed_sine, imag_part)
    mid_imag = from_left(cosine_table, imag_part) + from_left(signed_sine, real_part)
    out_real = from_right(mid_real, cosine_table) - from_right(mid_imag, signed_sine)
    out_imag = from_right(mid_imag, cosine_table) + from_right(mid_real, signed_sine)
    return (out_real, out_imag)


def propagate(real_part, imag_part, tables, kernel_real, kernel_imag):
    width_px = real_part.shape[-1]
    freq_real, freq_imag = transform(real_part, imag_part, tables, -1.0)
    next_real = kernel_real * freq_real - kernel_imag * freq_imag
    next_imag = kernel_real * freq_imag + kernel_imag * freq_real
    out_real, out_imag = transform(next_real, next_imag, tables, 1.0)
    scale = 1.0 / (width_px * width_px)
    return (out_real * scale, out_imag * scale)


def body(object_tiles, probe, measured, cover, counts, phase):
    width_px = probe.shape[-1]
    slot_count = measured.shape[0]
    scan_count = lax.axis_size("scan")
    device_index = lax.axis_index("scan")
    tables = dft_tables(width_px)
    own_tile = object_tiles[0]
    window_list = []
    for offset in range(-REACH, REACH + 1):
        if offset == 0:
            window_list.append(own_tile)
        else:
            window_list.append(passed_along(own_tile, "scan", -offset))
    window = jnp.stack(window_list)
    local_slot = cover - device_index + REACH
    patches = jnp.take(window, local_slot, axis=0)
    patch_real = patches[:, 0][:, None]
    patch_imag = patches[:, 1][:, None]
    probe_real = probe[:, 0][None]
    probe_imag = probe[:, 1][None]
    kernel_real = jnp.cos(phase)
    kernel_imag = jnp.sin(phase)
    exit_real = probe_real * patch_real - probe_imag * patch_imag
    exit_imag = probe_real * patch_imag + probe_imag * patch_real
    wave_real, wave_imag = propagate(exit_real, exit_imag, tables, kernel_real, kernel_imag)
    local_power = jnp.sum(wave_real * wave_real + wave_imag * wave_imag, axis=1)
    intensity = lax.psum(local_power, "mode")
    modulus = jnp.sqrt(intensity + 1.0)
    mismatch = modulus - measured
    slot_index = jnp.arange(slot_count, dtype=jnp.int32)
    alive_mask = (slot_index < counts[0]).astype(jnp.float32)
    weight = alive_mask[:, None, None] * mismatch / modulus
    back_real, back_imag = propagate(
        weight[:, None] * wave_real, weight[:, None] * wave_imag, tables, kernel_real, -kernel_imag
    )
    tile_real = jnp.sum(probe_real * back_real + probe_imag * back_imag, axis=1)
    tile_imag = jnp.sum(probe_real * back_imag - probe_imag * back_real, axis=1)
    tile_terms = jnp.stack([tile_real, tile_imag], axis=1)
    selector = (local_slot[:, None] == jnp.arange(2 * REACH + 1, dtype=jnp.int32)[None, :]).astype(
        jnp.float32
    )
    window_grad = jnp.einsum("pw,pcxy->wcxy", selector, tile_terms, precision=lax.Precision.HIGHEST)
    probe_real_grad = jnp.sum(patch_real * back_real + patch_imag * back_imag, axis=0)
    probe_imag_grad = jnp.sum(patch_real * back_imag - patch_imag * back_real, axis=0)
    probe_terms = jnp.stack([probe_real_grad, probe_imag_grad], axis=1)
    loss_terms = jnp.sum(alive_mask[:, None, None] * mismatch * mismatch)
    summed = lax.psum(window_grad, "mode")
    owned = summed[REACH]
    for offset in range(-REACH, REACH + 1):
        if offset != 0:
            owned = owned + passed_along(summed[REACH + offset], "scan", offset)
    probe_total, loss_total = lax.psum((probe_terms, loss_terms), "scan")
    loss = loss_total / (slot_count * scan_count * width_px * width_px)
    return (owned[None], probe_total, loss)


def solution(mesh):
    return jax.shard_map(
        body,
        mesh=mesh,
        in_specs=(
            P("scan", None, None, None),
            P("mode", None, None, None),
            P("scan", None, None),
            P("scan"),
            P("scan"),
            P(),
        ),
        out_specs=(P("scan", None, None, None), P("mode", None, None, None), P()),
        check_vma=False,
    )
```

profile of v0, /device:TPU:1, one launch (start us, length us, event | category | flops | bytes accessed | tf_op | source)
XLA Modules:
  0.0 508.8 jit_solution(2059840954880333223)
XLA Ops:
  7.2 0.0 all-reduce.4.cloned.1.call-start
  7.2 4.2 collective-permute-start
  11.4 4.0 collective-permute-start.1
  15.4 3.4 collective-permute-start.2
  18.8 1.3 collective-permute-start.3
  20.8 1.9 fusion.239
  22.7 0.0 copy-start
  22.7 6.3 %collective-permute-done.1 = f32[2,256,256]{2,1,0:T(8,128)S(1)} collective-permute-done((f32[2,256,256]{2,1,0:T(8,128)}, f32[2,256,256]{2,1,0:T(8,128)S(1)}, u32[]{:S(2)}, u32[]{:S(2)}) %collective-permute-start.1) | collective-permute-done | bytes 524320 | tf_op jit(solution)/shard_map/ppermute | solution.py:14
  29.1 0.0 collective-permute-done.2
  29.2 5.7 %collective-permute-done.3 = f32[2,256,256]{2,1,0:T(8,128)S(1)} collective-permute-done((f32[2,256,256]{2,1,0:T(8,128)}, f32[2,256,256]{2,1,0:T(8,128)S(1)}, u32[]{:S(2)}, u32[]{:S(2)}) %collective-permute-start.3) | collective-permute-done | bytes 524320 | tf_op jit(solution)/shard_map/ppermute | solution.py:14
  35.0 0.1 multiply_add_fusion.4
  35.1 1.5 fusion.24
  36.6 1.5 fusion.28
  38.0 1.5 fusion.12
  39.5 1.5 fusion.13
  41.0 1.5 fusion.79
  42.5 1.5 fusion.76
  44.0 1.5 convolution_subtract_fusion.6
  45.5 1.9 multiply_subtract_fusion.3
  47.3 1.5 fusion.74
  48.8 1.5 fusion.70
  50.3 1.5 fusion.11
  51.8 1.5 fusion.72
  53.2 1.5 fusion.10
  54.7 0.0 copy-start.2
  54.7 1.5 fusion.68
  56.2 1.5 fusion.9
  57.7 1.6 fusion.8
  59.3 0.7 add_bitcast_fusion
  60.1 0.0 all-reduce.4.cloned.1.call-update
  60.1 0.0 all-reduce.6.cloned.1.call-start
  60.8 56.1 %all-reduce.4.cloned.1.call-done = f32[1,256,256]{2,1,0:T(8,128)} async-done(((f32[1,256,256]{2,1,0:T(8,128)}), f32[1,256,256]{2,1,0:T(8,128)}) %all-reduce.4.cloned.1.call-update) | async-done | bytes 262160 | tf_op jit(solution)/shard_map/psum | solution.py:78
  116.9 1.7 fusion.20
  118.6 1.5 fusion.66
  120.1 1.5 fusion.62
  121.6 1.5 fusion.7
  123.1 1.5 fusion.6
  124.6 1.5 fusion.60
  126.0 1.5 fusion.64
  127.5 1.5 convolution_add_fusion.2
  129.0 1.7 multiply_add_fusion.2
  130.7 1.5 fusion.54
  132.2 1.5 fusion.58
  133.7 1.5 fusion.4
  135.2 1.5 fusion.5
  136.6 1.5 fusion.56
  138.1 1.5 fusion.52
  139.6 1.5 fusion.3
  141.0 1.5 multiply_add_fusion
  142.6 1.8 broadcast_multiply_fusion
  144.4 0.0 all-reduce.6.cloned.1.call-update
  144.5 0.0 all-reduce.8.cloned.1.call-start
  144.5 80.7 %all-reduce.6.cloned.1.call-done = f32[5,2,256,256]{3,2,1,0:T(8,128)} async-done(((f32[5,2,256,256]{3,2,1,0:T(8,128)}), f32[5,2,256,256]{3,2,1,0:T(8,128)}) %all-reduce.6.cloned.1.call-update) | async-done | bytes 2621456 | tf_op jit(solution)/shard_map/psum | solution.py:98
  225.2 2.7 slice_bitcast_fusion.3
  227.9 1.3 collective-permute-start.4
  229.2 2.6 collective-permute-start.5
  231.8 4.2 collective-permute-start.6
  236.0 3.1 collective-permute-start.7
  239.1 0.9 pad_maximum_fusion
  240.0 0.0 all-reduce.8.cloned.1.call-update
  240.0 256.2 %psum.31 = f32[]{:T(128)} all-reduce(f32[]{:T(128)} %get-tuple-element.28), channel_id=1, replica_groups=mesh['scan'=128,'mode'=4] {'scan'}, use_global_device_ids=true, to_apply=%region_4.5 | all-reduce | flops 1 | bytes 8 | tf_op jit(solution)/shard_map/psum | solution.py:103
  496.8 0.0 collective-permute-done.4
  496.9 2.0 fusion.18
  498.9 1.9 copy.18
  (17 shorter events, 0.3 us)
Async XLA Ops:
  7.2 21.9 %copy-start.1 = (f32[1,2,256,256]{3,2,1,0:T(8,128)S(1)}, f32[1,2,256,256]{3,2,1,0:T(8,128)}, u32[]{:S(2)}) copy-start(f32[1,2,256,256]{3,2,1,0:T(8,128)} %param.6) | copy-start | bytes 1572868
  7.2 109.7 %all-reduce.4.cloned.1.call-start = ((), (), s32[]{:S(2)}) async-start(), calls=%async_computation | async-start | bytes 524288 | tf_op jit(solution)/shard_map/psum | solution.py:78
  7.2 15.4 %collective-permute-start = (f32[2,256,256]{2,1,0:T(8,128)}, f32[2,256,256]{2,1,0:T(8,128)S(1)}, u32[]{:S(2)}, u32[]{:S(2)}) collective-permute-start(f32[2,256,256]{2,1,0:T(8,128)} %bitcast.130), channel_id=1, source_target_pairs={{0,8},{4,12},{8,16},{12,20},{16,24},{20,28},{24,32},{28,36},{32,40... | collective-permute-start | bytes 1572872 | tf_op jit(solution)/shard_map/ppermute | solution.py:14
  11.4 17.6 %collective-permute-start.1 = (f32[2,256,256]{2,1,0:T(8,128)}, f32[2,256,256]{2,1,0:T(8,128)S(1)}, u32[]{:S(2)}, u32[]{:S(2)}) collective-permute-start(f32[2,256,256]{2,1,0:T(8,128)} %bitcast.131), channel_id=1, source_target_pairs={{0,4},{4,8},{8,12},{12,16},{16,20},{20,24},{24,28},{28,32},{32,36}... | collective-permute-start | bytes 1572872 | tf_op jit(solution)/shard_map/ppermute | solution.py:14
  15.4 13.7 %collective-permute-start.2 = (f32[2,256,256]{2,1,0:T(8,128)}, f32[2,256,256]{2,1,0:T(8,128)S(1)}, u32[]{:S(2)}, u32[]{:S(2)}) collective-permute-start(f32[2,256,256]{2,1,0:T(8,128)} %bitcast.132), channel_id=1, source_target_pairs={{4,0},{8,4},{12,8},{16,12},{20,16},{24,20},{28,24},{32,28},{36,32}... | collective-permute-start | bytes 1572872 | tf_op jit(solution)/shard_map/ppermute | solution.py:14
  18.8 16.1 %collective-permute-start.3 = (f32[2,256,256]{2,1,0:T(8,128)}, f32[2,256,256]{2,1,0:T(8,128)S(1)}, u32[]{:S(2)}, u32[]{:S(2)}) collective-permute-start(f32[2,256,256]{2,1,0:T(8,128)} %bitcast.133), channel_id=1, source_target_pairs={{8,0},{12,4},{16,8},{20,12},{24,16},{28,20},{32,24},{36,28},{40,32... | collective-permute-start | bytes 1572872 | tf_op jit(solution)/shard_map/ppermute | solution.py:14
  22.7 12.3 %copy-start = (f32[1,2,256,256]{3,2,1,0:T(8,128)S(1)}, f32[1,2,256,256]{3,2,1,0:T(8,128)}, u32[]{:S(2)}) copy-start(f32[1,2,256,256]{3,2,1,0:T(8,128)} %param.7) | copy-start | bytes 1572868
  54.7 62.2 %copy-start.2 = (f32[1,256,256]{2,1,0:T(8,128)S(1)}, f32[1,256,256]{2,1,0:T(8,128)}, u32[]{:S(2)}) copy-start(f32[1,256,256]{2,1,0:T(8,128)} %param.8) | copy-start | bytes 786436
  60.1 165.1 %all-reduce.6.cloned.1.call-start = ((), (), s32[]{:S(2)}) async-start(), calls=%async_computation.1 | async-start | bytes 5242880 | tf_op jit(solution)/shard_map/psum | solution.py:98
  144.5 354.4 %all-reduce.8.cloned.1.call-start = ((), (), s32[]{:S(2)}) async-start(), calls=%async_computation.2 | async-start | bytes 1048576 | tf_op jit(solution)/shard_map/psum | solution.py:103
  227.9 268.9 %collective-permute-start.4 = (f32[2,256,256]{2,1,0:T(8,128)}, f32[2,256,256]{2,1,0:T(8,128)S(1)}, u32[]{:S(2)}, u32[]{:S(2)}) collective-permute-start(f32[2,256,256]{2,1,0:T(8,128)} %get-tuple-element.14), channel_id=1, source_target_pairs={{8,0},{12,4},{16,8},{20,12},{24,16},{28,20},{32,24},{36,28},{40,32... | collective-permute-start | bytes 1572872 | tf_op jit(solution)/shard_map/ppermute | solution.py:14
  229.2 267.6 %collective-permute-start.5 = (f32[2,256,256]{2,1,0:T(8,128)}, f32[2,256,256]{2,1,0:T(8,128)S(1)}, u32[]{:S(2)}, u32[]{:S(2)}) collective-permute-start(f32[2,256,256]{2,1,0:T(8,128)} %get-tuple-element.17), channel_id=1, source_target_pairs={{4,0},{8,4},{12,8},{16,12},{20,16},{24,20},{28,24},{32,28},{36,32}... | collective-permute-start | bytes 1572872 | tf_op jit(solution)/shard_map/ppermute | solution.py:14
  231.8 265.0 %collective-permute-start.6 = (f32[2,256,256]{2,1,0:T(8,128)}, f32[2,256,256]{2,1,0:T(8,128)S(1)}, u32[]{:S(2)}, u32[]{:S(2)}) collective-permute-start(f32[2,256,256]{2,1,0:T(8,128)} %get-tuple-element.16), channel_id=1, source_target_pairs={{0,4},{4,8},{8,12},{12,16},{16,20},{20,24},{24,28},{28,32},{32,36}... | collective-permute-start | bytes 1572872 | tf_op jit(solution)/shard_map/ppermute | solution.py:14
  236.0 260.9 %collective-permute-start.7 = (f32[2,256,256]{2,1,0:T(8,128)S(1)}, f32[2,256,256]{2,1,0:T(8,128)S(1)}, u32[]{:S(2)}, u32[]{:S(2)}) collective-permute-start(f32[2,256,256]{2,1,0:T(8,128)S(1)} %get-tuple-element.15), channel_id=1, source_target_pairs={{0,8},{4,12},{8,16},{12,20},{16,24},{20,28},{24,32},{28,36},{32,40... | collective-permute-start | bytes 1572872 | tf_op jit(solution)/shard_map/ppermute | solution.py:14
Sparse Core Ops, SparseCore 0:
  60.2 56.6 all-reduce.3
  144.6 80.5 all-reduce.5
  240.1 190.3 all-reduce.7
where the time goes:
time: 519 us; the launch traced here: 509 us
  blocking collectives  256 us (49%)
  waiting for transfers between devices  149 us (29%)
  matrix products  48 us (9%)
  starting transfers between devices  24.1 us (5%)
  between operations  17.7 us (3%)
  other arithmetic  7.24 us (1%)
  local copies, waits for them, and re-layouts  6.61 us (1%)
    psum x1, blocking collectives, body(): probe_total, loss_total = lax.psum((probe_terms, loss_terms), 'scan')  256 us
    psum x1, waiting for transfers between devices, body(): summed = lax.psum(window_grad, 'mode')  80.7 us
    psum x1, waiting for transfers between devices, body(): intensity = lax.psum(local_power, 'mode')  56.1 us
    dot_general x16, matrix products, from_right(): jnp.einsum('...jk,kl->...jl', field, matrix, precision=lax.Precision.HIGH...  24.3 us
    ppermute x8, starting transfers between devices, passed_along(): return lax.ppermute(block, axis, route)  24 us
    dot_general x16, matrix products, from_left(): jnp.einsum('ij,...jk->...ik', matrix, field, precision=lax.Precision.HIGH...  23.6 us
    ppermute x8, waiting for transfers between devices, passed_along(): return lax.ppermute(block, axis, route)  12.1 us
  transfers between devices with their start and end apart: 11, of which 4 were waited for; matrix products, arithmetic and copies ran while one was open for 1% of the time, Pallas kernels for 0%

commit v1 on v0

v1 whole, which is shorter than its diff:
```python
import functools
import math

import jax
import jax.numpy as jnp
import ml_dtypes
import numpy as np
from jax import lax
from jax.experimental import pallas as pl
from jax.experimental.pallas import tpu as pltpu
from jax.sharding import Mesh
from jax.sharding import PartitionSpec as P

REACH = 2
SCAN = ("z", "y", "core")
PLANE = ("z", "y")
VMEM = pl.BlockSpec(memory_space=pltpu.VMEM)
SMEM = pl.BlockSpec(memory_space=pltpu.SMEM)
FLAG_ROWS = 8


def moved(block, axis, distance):
    size = lax.axis_size(axis)
    return lax.ppermute(block, axis, [(i, (i + distance) % size) for i in range(size)])


def split_tables(width):
    half = width // 2
    freq, place = np.arange(half)[:, None], np.arange(half)[None, :]
    out = []
    for parity in (0, 1):
        angle = ((2 * freq + parity) * place % width) * (2.0 * np.pi / width)
        cosine, sine = np.cos(angle), np.sin(angle)
        real_form = np.block([[cosine, sine], [-sine, cosine]])
        high = real_form.astype(np.float32).astype(ml_dtypes.bfloat16)
        low = (real_form - high.astype(np.float64)).astype(np.float32).astype(ml_dtypes.bfloat16)
        out += [high, low, np.ascontiguousarray(high.T), np.ascontiguousarray(low.T)]
    return np.stack(out)


def permutation(width):
    half = width // 2
    matrix = np.zeros((width, width), np.float32)
    for parity in (0, 1):
        for index in range(half):
            matrix[2 * index + parity, parity * half + index] = 1.0
    return np.stack([matrix, matrix.T]).astype(ml_dtypes.bfloat16)


def halves(value):
    high = value.astype(jnp.bfloat16)
    return high, (value - high.astype(jnp.float32)).astype(jnp.bfloat16)


def dot(left, right):
    return jnp.dot(left, right, preferred_element_type=jnp.float32)


def table_times(high, low, field):
    field_high, field_low = halves(field)
    return dot(
        jnp.concatenate([high, high, low], axis=1),
        jnp.concatenate([field_high, field_low, field_high], axis=0),
    )


def times_table(field, high, low):
    field_high, field_low = halves(field)
    return dot(
        jnp.concatenate([field_high, field_low, field_high], axis=1),
        jnp.concatenate([high, high, low], axis=0),
    )


def rows(*blocks):
    return jnp.concatenate(blocks, axis=0)


def cols(*blocks):
    return jnp.concatenate(blocks, axis=1)


def propagated(real, imag, tables, kernel):
    half = real.shape[0] // 2
    top, bottom = slice(0, half), slice(half, 2 * half)
    sums = rows(real[top] + real[bottom], imag[top] + imag[bottom])
    diffs = rows(real[top] - real[bottom], imag[top] - imag[bottom])
    bands = [
        table_times(tables[4 * p], tables[4 * p + 1], part) for p, part in ((0, sums), (1, diffs))
    ]
    left, right = slice(0, half), slice(half, 2 * half)
    plus = rows(*[cols(b[top, left] + b[top, right], b[bottom, left] + b[bottom, right]) for b in bands])
    minus = rows(*[cols(b[top, left] - b[top, right], b[bottom, left] - b[bottom, right]) for b in bands])
    back = []
    for q, part in ((0, plus), (1, minus)):
        freq = times_table(part, tables[4 * q + 2], tables[4 * q + 3])
        freq_real, freq_imag = freq[:, left], freq[:, right]
        kernel_real, kernel_imag = kernel(q)
        turned = cols(
            kernel_real * freq_real - kernel_imag * freq_imag,
            kernel_real * freq_imag + kernel_imag * freq_real,
        )
        back.append(times_table(turned, tables[4 * q], tables[4 * q + 1]))
    total, gap = back[0] + back[1], back[0] - back[1]
    out = []
    for p, band in ((0, top), (1, bottom)):
        stacked = rows(cols(total[band, left], gap[band, left]), cols(total[band, right], gap[band, right]))
        out.append(table_times(tables[4 * p + 2], tables[4 * p + 3], stacked))
    total, gap = out[0] + out[1], out[0] - out[1]
    return rows(total[top], gap[top]), rows(total[bottom], gap[bottom])


SIN_TERMS = [(-1.0) ** k / math.factorial(2 * k + 1) for k in range(7)]
COS_TERMS = [(-1.0) ** k / math.factorial(2 * k) for k in range(8)]


def horner(terms, square):
    total = jnp.full_like(square, terms[-1])
    for term in terms[-2::-1]:
        total = total * square + term
    return total


def cos_sin(phase):
    angle = phase * 0.5
    square = angle * angle
    sine = angle * horner(SIN_TERMS, square)
    cosine = horner(COS_TERMS, square)
    return 1.0 - 2.0 * sine * sine, 2.0 * sine * cosine


def forward_kernel(tile, probe, phase, tables, order, wave, power, turn):
    width = phase.shape[-1]
    half = width // 2
    scale = 1.0 / (width * width)
    rest = phase[...]
    ordered = None
    for _ in range(3):
        piece = rest.astype(jnp.bfloat16)
        rest = rest - piece.astype(jnp.float32)
        piece = dot(order[1], dot(piece, order[0]).astype(jnp.bfloat16))
        ordered = piece if ordered is None else ordered + piece
    cosine, sine = cos_sin(ordered)
    turn[0] = cosine * scale
    turn[1] = sine * scale
    exit_real = probe[0] * tile[0] - probe[1] * tile[1]
    exit_imag = probe[0] * tile[1] + probe[1] * tile[0]

    def kernel(q):
        lanes = slice(q * half, q * half + half)
        return turn[0, :, lanes], turn[1, :, lanes]

    real, imag = propagated(exit_real, exit_imag, [tables[i] for i in range(8)], kernel)
    wave[0] = real
    wave[1] = imag
    power[...] = real * real + imag * imag


def backward_kernel(
    place, tile, probe, wave, turn, tables, own, one, two, three, slot, *refs
):
    slots, (keep, send, tile_terms) = (slot,) + refs[: 2 * REACH], refs[2 * REACH :]
    width = own.shape[-1]
    half = width // 2
    home = place[0].astype(jnp.float32)
    core = place[1]
    intensity = (own[...] + one[...]) + (two[...] + three[...])
    modulus = jnp.sqrt(intensity + 1.0)
    mismatch_sum = jnp.zeros_like(modulus)
    squares = jnp.zeros_like(modulus)
    for ref in slots:
        chosen = (ref[width : width + 1, :] == home).astype(jnp.float32)
        mismatch = chosen * (modulus - ref[:width, :])
        mismatch_sum += mismatch
        squares += mismatch * mismatch
    weight = mismatch_sum / modulus

    def kernel(q):
        lanes = slice(q * half, q * half + half)
        return turn[0, :, lanes], -turn[1, :, lanes]

    real, imag = propagated(weight * wave[0], weight * wave[1], [tables[i] for i in range(8)], kernel)
    tile_terms[0] = probe[0] * real + probe[1] * imag
    tile_terms[1] = probe[0] * imag - probe[1] * real
    terms = (tile[0] * real + tile[1] * imag, tile[0] * imag - tile[1] * real)
    chunks = keep.shape[0] // 16 - 1
    first = core == 0
    for side in (0, 1):
        lanes = slice(side * half, side * half + half)
        for ref, value in (
            (keep, jnp.where(first, terms[0][:, lanes], terms[1][:, lanes])),
            (send, jnp.where(first, terms[1][:, lanes], terms[0][:, lanes])),
        ):
            ref[side * width : (side + 1) * width, :] = value
    loss = jnp.full((8, 128), jnp.sum(squares))
    keep[2 * width :, :] = loss
    send[2 * width :, :] = loss


def pair_kernel(keep, received, chunks):
    total = keep[...] + received[...]
    count = chunks.shape[0]
    chunks[:, 0:8, :] = total[: 8 * count].reshape(count, 8, 128)
    chunks[:, 8:16, :] = jnp.broadcast_to(total[8 * count :][None], (count, 8, 128))


def gather_kernel(arrived, spread, loss):
    total = jnp.sum(arrived[...], axis=0)
    spread[...] = jnp.broadcast_to(total[None, :8], spread.shape)
    loss[...] = total[8:]


def finish_kernel(place, mine, other, objects, probe_total, object_total):
    first = place[1] == 0
    width = probe_total.shape[-1]
    half = width // 2
    blocks = mine.shape[0] // 2
    for side in (0, 1):
        lanes = slice(side * half, side * half + half)
        here = mine[side * blocks : (side + 1) * blocks].reshape(width, half)
        there = other[side * blocks : (side + 1) * blocks].reshape(width, half)
        probe_total[0, 0, :, lanes] = jnp.where(first, here, there)
        probe_total[0, 1, :, lanes] = jnp.where(first, there, here)
    object_total[0] = (objects[0] + objects[1]) + (objects[2] + objects[3])


def struct(*shape):
    return jax.ShapeDtypeStruct(shape, jnp.float32)


def call(kernel, outs, name, scalars=0, operands=0):
    return pl.pallas_call(
        kernel,
        out_shape=outs,
        in_specs=[SMEM] * scalars + [VMEM] * operands,
        out_specs=jax.tree.map(lambda _: VMEM, outs),
        compiler_params=pltpu.CompilerParams(vmem_limit_bytes=24 * 1024 * 1024),
        name=name,
    )


def body(scan_size, object_tiles, probe, measured, cover, counts, phase):
    width = phase.shape[-1]
    tables = jnp.asarray(split_tables(width))
    order = jnp.asarray(permutation(width))
    home = lax.axis_index(SCAN)
    place = jnp.stack([home + 1, lax.axis_index("core")]).astype(jnp.int32)
    marker = jnp.where(counts[0] > 0, cover[0] + 1, 0).astype(jnp.float32)
    slot = jnp.concatenate([measured[0], jnp.broadcast_to(marker, (FLAG_ROWS, width))])
    around = [
        lax.ppermute(slot, SCAN, [(i, (i + d) % scan_size) for i in range(scan_size)])
        for d in range(-REACH, REACH + 1)
        if d
    ]
    wave, power, turn = call(
        forward_kernel,
        (struct(2, width, width), struct(width, width), struct(2, width, width)),
        "forward",
        operands=5,
    )(object_tiles[0], probe[0], phase, tables, order)
    powers = [moved(power, "mode", d) for d in (1, 2, 3)]
    keep, send, tile_terms = call(
        backward_kernel,
        (struct(2 * width + 8, 128), struct(2 * width + 8, 128), struct(2, width, width)),
        "backward",
        scalars=1,
        operands=10 + 2 * REACH,
    )(place, object_tiles[0], probe[0], wave, turn, tables, power, *powers, slot, *around)
    objects = lax.all_gather(tile_terms, "mode")
    received = moved(send, "core", 1)
    peers = lax.axis_size(PLANE)
    chunks = call(pair_kernel, struct(peers, 16, 128), "pair", operands=2)(keep, received)
    arrived = lax.all_to_all(chunks, PLANE, 0, 0, tiled=True)
    spread, loss = call(
        gather_kernel, (struct(peers, 8, 128), struct(8, 128)), "gather", operands=1
    )(arrived)
    mine = lax.all_to_all(spread, PLANE, 0, 0, tiled=True)
    other = moved(mine, "core", 1)
    probe_total, object_total = call(
        finish_kernel,
        (struct(1, 2, width, width), struct(1, 2, width, width)),
        "finish",
        scalars=1,
        operands=3,
    )(place, mine, other, objects)
    return object_total, probe_total, loss[0, 0] / (scan_size * width * width)


def solution(mesh):
    scan_size, modes = mesh.shape["scan"], mesh.shape["mode"]
    cube = Mesh(mesh.devices.reshape(8, 8, 2, modes), ("z", "y", "core", "mode"))
    return jax.shard_map(
        functools.partial(body, scan_size),
        mesh=cube,
        in_specs=(
            P(SCAN, None, None, None),
            P("mode", None, None, None),
            P(SCAN, None, None),
            P(SCAN),
            P(SCAN),
            P(),
        ),
        out_specs=(P(SCAN, None, None, None), P("mode", None, None, None), P()),
        check_vma=False,
    )
```

time: 519 us -> 133 us (0.26); the launches traced: 509 us -> 132 us
  blocking collectives: 256 us -> 43.4 us
  waiting for transfers between devices: 149 us -> 9.2 us
  matrix products: 48 us -> 0 us
  starting transfers between devices: 24.1 us -> 40.5 us
  Pallas kernels: 0 us -> 7.99 us
  local copies, waits for them, and re-layouts: 6.61 us -> 13.8 us
  other arithmetic: 7.24 us -> 0.08 us
    psum x1 -> x0, blocking collectives: 256 us -> none  [body(): probe_total, loss_total = lax.psum((probe_terms, loss_terms), 'scan')]
    psum x3 -> x0, waiting for transfers between devices: 137 us -> none  [the longest x1 80.7 us: body(): summed = lax.psum(window_grad, 'mode')]
    dot_general x32 -> x0, matrix products: 48 us -> none  [the longest x16 24.3 us: from_right(): jnp.einsum('...jk,kl->...jl', field, matrix, precision=lax.Precision.HIGH...]
    all_to_all x0 -> x2, blocking collectives: none -> 43.4 us  [the longest x1 24.5 us: body(): arrived = lax.all_to_all(chunks, PLANE, 0, 0, tiled=True)]
    ppermute x8 -> x9, starting transfers between devices: 24 us -> 40.4 us  [the longest x4 20.6 us: body(): lax.ppermute(slot, SCAN, [(i, (i + d) % scan_size) for i in range(scan_si...]
    unnamed x11 -> x36, local copies, waits for them, and re-layouts: 2.03 us -> 13.2 us
    pallas_call x0 -> x5, Pallas kernels: none -> 7.99 us  [the longest x1 3.36 us: body(): call(backward_kernel, (struct(2 * width + 8, 128), struct(2 * width + 8,...]
    ppermute x8 -> x9, waiting for transfers between devices: 12.1 us -> 9.16 us  [the longest x5 9.15 us: moved(): lax.ppermute(block, axis, [(i, (i + distance) % size) for i in range(size)])]
  transfers between devices with their start and end apart: 11 -> 10, of which waited for: 4 -> 2; matrix products, arithmetic and copies ran while one was open for 1% -> 0% of each run, Pallas kernels for 0% -> 0%
where the time goes in v1:
time: 133 us; the launch traced here: 132 us
  blocking collectives  43.4 us (33%)
  starting transfers between devices  40.5 us (30%)
  between operations  17.4 us (13%)
  local copies, waits for them, and re-layouts  13.8 us (10%)
  waiting for transfers between devices  9.2 us (7%)
  Pallas kernels  7.99 us (6%)
    all_to_all x1, blocking collectives, body(): arrived = lax.all_to_all(chunks, PLANE, 0, 0, tiled=True)  24.5 us
    ppermute x4, starting transfers between devices, body(): lax.ppermute(slot, SCAN, [(i, (i + d) % scan_size) for i in range(scan_si...  20.6 us
    ppermute x5, starting transfers between devices, moved(): lax.ppermute(block, axis, [(i, (i + distance) % size) for i in range(size)])  19.9 us
    all_to_all x1, blocking collectives, body(): mine = lax.all_to_all(spread, PLANE, 0, 0, tiled=True)  18.9 us
    unnamed x36, local copies, waits for them, and re-layouts  13.2 us
    ppermute x5, waiting for transfers between devices, moved(): lax.ppermute(block, axis, [(i, (i + distance) % size) for i in range(size)])  9.15 us
    pallas_call x1, Pallas kernels, body(): call(backward_kernel, (struct(2 * width + 8, 128), struct(2 * width + 8,...  3.36 us
    pallas_call x1, Pallas kernels, body(): call(forward_kernel, (struct(2, width, width), struct(width, width), stru...  2.85 us
  transfers between devices with their start and end apart: 10, of which 2 were waited for; matrix products, arithmetic and copies ran while one was open for 0% of the time, Pallas kernels for 0%

profile of v1, /device:TPU:1, one launch (start us, length us, event | category | flops | bytes accessed | tf_op | source)
XLA Modules:
  0.0 132.3 jit_solution(17338421242713805097)
XLA Ops:
  7.2 0.0 all-gather.3.cloned.1.call-start
  7.2 0.0 copy-start
  7.2 1.2 copy-done
  8.4 1.0 copy-done.2
  9.5 0.0 copy-start.4
  9.5 1.0 copy-done.4
  10.5 0.0 copy-start.10
  10.5 0.9 copy-done.10
  11.5 0.0 copy-start.15
  11.5 0.9 copy-done.15
  12.4 0.0 copy-start.17
  12.4 0.0 copy-start.1
  12.4 0.0 copy-start.3
  12.4 0.0 copy-start.5
  12.4 2.8 %forward.1 = (f32[2,256,256]{2,1,0:T(8,128)S(1)}, f32[256,256]{1,0:T(8,128)}, f32[2,256,256]{2,1,0:T(8,128)S(1)}) custom-call(f32[2,256,256]{2,1,0:T(8,128)S(1)} %bitcast.8, f32[2,256,256]{2,1,0:T(8,128)S(1)} %bitcast.10, f32[256,256]{1,0:T(8,128)S(1)} %copy-done.10, bf16[8,256,256]{2,1,0:T(8,128)(2,1)S(1)} %copy-done, bf16[2,256,256]{2,1,0:T(8,128)(2,1)S(1)} %copy-done.15), custom_call_target="tpu_custom_call" | custom-call | tf_op jit(solution)/shard_map/forward/pallas_call | solution.py:255
  15.3 5.2 %collective-permute-start.2 = (f32[256,256]{1,0:T(8,128)}, f32[256,256]{1,0:T(8,128)S(1)}, u32[]{:S(2)}, u32[]{:S(2)}) collective-permute-start(f32[256,256]{1,0:T(8,128)} %get-tuple-element.15.own), channel_id=1, source_target_pairs={{0,3},{1,0},{2,1},{3,2},{4,7},{5,4},{6,5},{7,6},{8,11},{9,8},{10,9... | collective-permute-start | bytes 786440 | tf_op jit(solution)/shard_map/ppermute | solution.py:24
  20.5 2.4 %collective-permute-start.1 = (f32[256,256]{1,0:T(8,128)}, f32[256,256]{1,0:T(8,128)S(1)}, u32[]{:S(2)}, u32[]{:S(2)}) collective-permute-start(f32[256,256]{1,0:T(8,128)} %get-tuple-element.15.own), channel_id=1, source_target_pairs={{0,2},{1,3},{2,0},{3,1},{4,6},{5,7},{6,4},{7,5},{8,10},{9,11},{10,... | collective-permute-start | bytes 786440 | tf_op jit(solution)/shard_map/ppermute | solution.py:24
  24.2 0.0 copy-done.17
  24.3 3.2 %collective-permute-start.6 = (f32[264,256]{1,0:T(8,128)S(1)}, f32[264,256]{1,0:T(8,128)}, u32[]{:S(2)}, u32[]{:S(2)}) collective-permute-start(f32[264,256]{1,0:T(8,128)S(1)} %concatenate.3.slot), channel_id=1, source_target_pairs={{0,8},{4,12},{8,16},{12,20},{16,24},{20,28},{24,32},{28,36},{32,40... | collective-permute-start | bytes 811016 | tf_op jit(solution)/shard_map/ppermute | solution.py:251
  27.5 4.6 %collective-permute-start.5 = (f32[264,256]{1,0:T(8,128)S(1)}, f32[264,256]{1,0:T(8,128)}, u32[]{:S(2)}, u32[]{:S(2)}) collective-permute-start(f32[264,256]{1,0:T(8,128)S(1)} %concatenate.3.slot), channel_id=1, source_target_pairs={{0,4},{4,8},{8,12},{12,16},{16,20},{20,24},{24,28},{28,32},{32,36}... | collective-permute-start | bytes 811016 | tf_op jit(solution)/shard_map/ppermute | solution.py:251
  32.1 1.9 %collective-permute-start.4 = (f32[264,256]{1,0:T(8,128)S(1)}, f32[264,256]{1,0:T(8,128)}, u32[]{:S(2)}, u32[]{:S(2)}) collective-permute-start(f32[264,256]{1,0:T(8,128)S(1)} %concatenate.3.slot), channel_id=1, source_target_pairs={{0,508},{4,0},{8,4},{12,8},{16,12},{20,16},{24,20},{28,24},{32,28}... | collective-permute-start | bytes 811016 | tf_op jit(solution)/shard_map/ppermute | solution.py:251
  34.0 0.0 collective-permute-done.2.three
  34.0 0.0 copy-start.11
  34.0 0.7 copy-done.11
  34.7 10.8 %collective-permute-start.3 = (f32[264,256]{1,0:T(8,128)S(1)}, f32[264,256]{1,0:T(8,128)}, u32[]{:S(2)}, u32[]{:S(2)}) collective-permute-start(f32[264,256]{1,0:T(8,128)S(1)} %concatenate.3.slot), channel_id=1, source_target_pairs={{0,504},{4,508},{8,0},{12,4},{16,8},{20,12},{24,16},{28,20},{32,24... | collective-permute-start | bytes 811016 | tf_op jit(solution)/shard_map/ppermute | solution.py:251
  45.5 0.0 collective-permute-done.1.two
  45.6 0.0 copy-start.13
  45.6 0.7 copy-done.13
  46.3 2.5 %collective-permute-start = (f32[256,256]{1,0:T(8,128)}, f32[256,256]{1,0:T(8,128)}, u32[]{:S(2)}, u32[]{:S(2)}) collective-permute-start(f32[256,256]{1,0:T(8,128)} %get-tuple-element.15.own), channel_id=1, source_target_pairs={{0,1},{1,2},{2,3},{3,0},{4,5},{5,6},{6,7},{7,4},{8,9},{9,10},{10,1... | collective-permute-start | bytes 786440 | tf_op jit(solution)/shard_map/ppermute | solution.py:24
  48.8 0.1 pad_add_fusion.place
  48.9 7.8 %collective-permute-done.one = f32[256,256]{1,0:T(8,128)} collective-permute-done((f32[256,256]{1,0:T(8,128)}, f32[256,256]{1,0:T(8,128)}, u32[]{:S(2)}, u32[]{:S(2)}) %collective-permute-start) | collective-permute-done | bytes 262176 | tf_op jit(solution)/shard_map/ppermute | solution.py:24
  56.6 0.0 collective-permute-done.6.refs_3_
  56.7 0.0 collective-permute-done.5.refs_2_
  56.7 0.0 collective-permute-done.4.refs_1_
  56.7 0.0 collective-permute-done.3.refs_0_
  56.7 0.0 copy-done.1
  56.7 0.0 copy-done.3
  56.7 0.0 copy-done.5
  56.7 0.0 copy-start.12
  56.7 0.9 copy-done.12
  57.7 0.0 copy-start.14
  57.7 0.9 copy-done.14
  58.6 3.4 %backward.1 = (f32[520,128]{1,0:T(8,128)S(1)}, f32[520,128]{1,0:T(8,128)S(1)}, f32[2,256,256]{2,1,0:T(8,128)S(1)}) custom-call(s32[2]{0:T(128)S(1)} %pad_add_fusion.place, f32[2,256,256]{2,1,0:T(8,128)S(1)} %bitcast.9, f32[2,256,256]{2,1,0:T(8,128)S(1)} %bitcast.11, f32[2,256,256]{2,1,0:T(8,128)S(1)} %get-tuple-element.13.wave, ...), custom_call_target="tpu_custom_call" | custom-call | tf_op jit(solution)/shard_map/backward/pallas_call | solution.py:262
  62.0 0.0 copy-start.7
  62.0 0.8 copy-done.7
  62.8 0.7 copy-done.8
  63.5 0.0 copy-start.16
  63.5 0.7 copy-done.16
  64.2 0.0 all-gather.3.cloned.1.call-update
  64.2 4.4 %collective-permute-start.7 = (f32[520,128]{1,0:T(8,128)}, f32[520,128]{1,0:T(8,128)S(1)}, u32[]{:S(2)}, u32[]{:S(2)}) collective-permute-start(f32[520,128]{1,0:T(8,128)} %copy-done.16), channel_id=1, source_target_pairs={{0,4},{4,0},{1,5},{5,1},{2,6},{6,2},{3,7},{7,3},{8,12},{12,8},{9,1... | collective-permute-start | bytes 798728 | tf_op jit(solution)/shard_map/ppermute | solution.py:24
  68.6 1.4 %collective-permute-done.7.received = f32[520,128]{1,0:T(8,128)S(1)} collective-permute-done((f32[520,128]{1,0:T(8,128)}, f32[520,128]{1,0:T(8,128)S(1)}, u32[]{:S(2)}, u32[]{:S(2)}) %collective-permute-start.7) | collective-permute-done | bytes 266272 | tf_op jit(solution)/shard_map/ppermute | solution.py:24
  70.0 0.0 copy-start.9
  70.0 0.9 copy-done.9
  70.9 0.1 pair.1
  71.0 24.5 %all_to_all.10.arrived = f32[64,16,128]{2,1,0:T(8,128)S(1)} all-to-all(f32[64,16,128]{2,1,0:T(8,128)S(1)} %pair.1), channel_id=1, replica_groups=mesh['z'=8,'y'=8,'core'=2,'mode'=4] {'z','y'}, dimensions={0} | all-to-all | bytes 1048576 | tf_op jit(solution)/shard_map/all_to_all | solution.py:273
  95.5 0.1 gather.1
  95.6 18.9 %all_to_all.11.mine = f32[64,8,128]{2,1,0:T(8,128)S(1)} all-to-all(f32[64,8,128]{2,1,0:T(8,128)S(1)} %get-tuple-element.18), channel_id=1, replica_groups=mesh['z'=8,'y'=8,'core'=2,'mode'=4] {'z','y'}, dimensions={0} | all-to-all | bytes 524288 | tf_op jit(solution)/shard_map/all_to_all | solution.py:277
  114.5 5.4 %collective-permute-start.8 = (f32[64,8,128]{2,1,0:T(8,128)S(1)}, f32[64,8,128]{2,1,0:T(8,128)S(1)}, u32[]{:S(2)}, u32[]{:S(2)}) collective-permute-start(f32[64,8,128]{2,1,0:T(8,128)S(1)} %all_to_all.11.mine), channel_id=1, source_target_pairs={{0,4},{4,0},{1,5},{5,1},{2,6},{6,2},{3,7},{7,3},{8,12},{12,8},{9,1... | collective-permute-start | bytes 786440 | tf_op jit(solution)/shard_map/ppermute | solution.py:24
  119.9 0.5 slice.3
  121.0 0.0 collective-permute-done.8.other
  121.0 0.0 all-gather.3.cloned.1.call-done
  121.1 0.0 copy-start.6
  121.1 1.6 %copy-done.6 = f32[8,256,256]{2,1,0:T(8,128)S(1)} copy-done((f32[8,256,256]{2,1,0:T(8,128)S(1)}, f32[8,256,256]{2,1,0:T(8,128)}, u32[]{:S(2)}) %copy-start.6) | copy-done | bytes 2097176
  122.7 1.6 %finish.1 = (f32[1,2,256,256]{3,2,1,0:T(8,128)}, f32[1,2,256,256]{3,2,1,0:T(8,128)}) custom-call(s32[2]{0:T(128)S(1)} %pad_add_fusion.place, f32[64,8,128]{2,1,0:T(8,128)S(1)} %all_to_all.11.mine, f32[64,8,128]{2,1,0:T(8,128)S(1)} %collective-permute-done.8.other, f32[4,2,256,256]{3,2,1,0:T(8,128)S(1)} %bitcast.12), custom_call_target="tpu_custom_call" | custom-call | tf_op jit(solution)/shard_map/finish/pallas_call | solution.py:279
  (3 shorter events, 0.0 us)
Async XLA Ops:
  7.2 113.9 %all-gather.3.cloned.1.call-start = ((), (), s32[]{:S(2)}) async-start(), calls=%async_computation.2 | async-start | bytes 2621440 | tf_op jit(solution)/shard_map/all_gather | solution.py:269
  7.2 1.2 copy-start
  8.4 1.0 copy-start.2
  9.5 1.0 copy-start.4
  10.5 0.9 copy-start.10
  11.5 0.9 copy-start.15
  12.4 11.8 %copy-start.17 = (f32[1,256,256]{2,1,0:T(8,128)S(1)}, f32[1,256,256]{2,1,0:T(8,128)}, u32[]{:S(2)}) copy-start(f32[1,256,256]{2,1,0:T(8,128)} %param.10) | copy-start | bytes 786436
  12.4 44.2 %copy-start.1 = (bf16[8,256,256]{2,1,0:T(8,128)(2,1)S(1)}, bf16[8,256,256]{2,1,0:T(8,128)(2,1)}, u32[]{:S(2)}) copy-start(bf16[8,256,256]{2,1,0:T(8,128)(2,1)} %constant.35.clone.tables) | copy-start | bytes 3145732
  12.4 44.3 %copy-start.3 = (f32[1,2,256,256]{3,2,1,0:T(8,128)S(1)}, f32[1,2,256,256]{3,2,1,0:T(8,128)}, u32[]{:S(2)}) copy-start(f32[1,2,256,256]{3,2,1,0:T(8,128)} %param.8) | copy-start | bytes 1572868
  12.4 44.3 %copy-start.5 = (f32[1,2,256,256]{3,2,1,0:T(8,128)S(1)}, f32[1,2,256,256]{3,2,1,0:T(8,128)}, u32[]{:S(2)}) copy-start(f32[1,2,256,256]{3,2,1,0:T(8,128)} %param.9) | copy-start | bytes 1572868
  15.3 18.7 %collective-permute-start.2 = (f32[256,256]{1,0:T(8,128)}, f32[256,256]{1,0:T(8,128)S(1)}, u32[]{:S(2)}, u32[]{:S(2)}) collective-permute-start(f32[256,256]{1,0:T(8,128)} %get-tuple-element.15.own), channel_id=1, source_target_pairs={{0,3},{1,0},{2,1},{3,2},{4,7},{5,4},{6,5},{7,6},{8,11},{9,8},{10,9... | collective-permute-start | bytes 786440 | tf_op jit(solution)/shard_map/ppermute | solution.py:24
  20.5 25.1 %collective-permute-start.1 = (f32[256,256]{1,0:T(8,128)}, f32[256,256]{1,0:T(8,128)S(1)}, u32[]{:S(2)}, u32[]{:S(2)}) collective-permute-start(f32[256,256]{1,0:T(8,128)} %get-tuple-element.15.own), channel_id=1, source_target_pairs={{0,2},{1,3},{2,0},{3,1},{4,6},{5,7},{6,4},{7,5},{8,10},{9,11},{10,... | collective-permute-start | bytes 786440 | tf_op jit(solution)/shard_map/ppermute | solution.py:24
  24.3 32.4 %collective-permute-start.6 = (f32[264,256]{1,0:T(8,128)S(1)}, f32[264,256]{1,0:T(8,128)}, u32[]{:S(2)}, u32[]{:S(2)}) collective-permute-start(f32[264,256]{1,0:T(8,128)S(1)} %concatenate.3.slot), channel_id=1, source_target_pairs={{0,8},{4,12},{8,16},{12,20},{16,24},{20,28},{24,32},{28,36},{32,40... | collective-permute-start | bytes 811016 | tf_op jit(solution)/shard_map/ppermute | solution.py:251
  27.5 29.2 %collective-permute-start.5 = (f32[264,256]{1,0:T(8,128)S(1)}, f32[264,256]{1,0:T(8,128)}, u32[]{:S(2)}, u32[]{:S(2)}) collective-permute-start(f32[264,256]{1,0:T(8,128)S(1)} %concatenate.3.slot), channel_id=1, source_target_pairs={{0,4},{4,8},{8,12},{12,16},{16,20},{20,24},{24,28},{28,32},{32,36}... | collective-permute-start | bytes 811016 | tf_op jit(solution)/shard_map/ppermute | solution.py:251
  32.1 24.6 %collective-permute-start.4 = (f32[264,256]{1,0:T(8,128)S(1)}, f32[264,256]{1,0:T(8,128)}, u32[]{:S(2)}, u32[]{:S(2)}) collective-permute-start(f32[264,256]{1,0:T(8,128)S(1)} %concatenate.3.slot), channel_id=1, source_target_pairs={{0,508},{4,0},{8,4},{12,8},{16,12},{20,16},{24,20},{28,24},{32,28}... | collective-permute-start | bytes 811016 | tf_op jit(solution)/shard_map/ppermute | solution.py:251
  34.0 0.7 copy-start.11
  34.7 21.9 %collective-permute-start.3 = (f32[264,256]{1,0:T(8,128)S(1)}, f32[264,256]{1,0:T(8,128)}, u32[]{:S(2)}, u32[]{:S(2)}) collective-permute-start(f32[264,256]{1,0:T(8,128)S(1)} %concatenate.3.slot), channel_id=1, source_target_pairs={{0,504},{4,508},{8,0},{12,4},{16,8},{20,12},{24,16},{28,20},{32,24... | collective-permute-start | bytes 811016 | tf_op jit(solution)/shard_map/ppermute | solution.py:251
  45.6 0.7 copy-start.13
  46.3 10.4 %collective-permute-start = (f32[256,256]{1,0:T(8,128)}, f32[256,256]{1,0:T(8,128)}, u32[]{:S(2)}, u32[]{:S(2)}) collective-permute-start(f32[256,256]{1,0:T(8,128)} %get-tuple-element.15.own), channel_id=1, source_target_pairs={{0,1},{1,2},{2,3},{3,0},{4,5},{5,6},{6,7},{7,4},{8,9},{9,10},{10,1... | collective-permute-start | bytes 786440 | tf_op jit(solution)/shard_map/ppermute | solution.py:24
  56.7 1.0 copy-start.12
  57.7 0.9 copy-start.14
  62.0 0.8 copy-start.7
  62.8 0.7 copy-start.8
  63.5 0.7 copy-start.16
  64.2 5.7 %collective-permute-start.7 = (f32[520,128]{1,0:T(8,128)}, f32[520,128]{1,0:T(8,128)S(1)}, u32[]{:S(2)}, u32[]{:S(2)}) collective-permute-start(f32[520,128]{1,0:T(8,128)} %copy-done.16), channel_id=1, source_target_pairs={{0,4},{4,0},{1,5},{5,1},{2,6},{6,2},{3,7},{7,3},{8,12},{12,8},{9,1... | collective-permute-start | bytes 798728 | tf_op jit(solution)/shard_map/ppermute | solution.py:24
  70.0 1.0 copy-start.9
  114.5 6.5 %collective-permute-start.8 = (f32[64,8,128]{2,1,0:T(8,128)S(1)}, f32[64,8,128]{2,1,0:T(8,128)S(1)}, u32[]{:S(2)}, u32[]{:S(2)}) collective-permute-start(f32[64,8,128]{2,1,0:T(8,128)S(1)} %all_to_all.11.mine), channel_id=1, source_target_pairs={{0,4},{4,0},{1,5},{5,1},{2,6},{6,2},{3,7},{7,3},{8,12},{12,8},{9,1... | collective-permute-start | bytes 786440 | tf_op jit(solution)/shard_map/ppermute | solution.py:24
  121.1 1.6 %copy-start.6 = (f32[8,256,256]{2,1,0:T(8,128)S(1)}, f32[8,256,256]{2,1,0:T(8,128)}, u32[]{:S(2)}) copy-start(f32[8,256,256]{2,1,0:T(8,128)} %all-gather.3.cloned.1.call-done) | copy-start | bytes 6291460
Sparse Core Ops, SparseCore 0:
  64.3 31.9 all-gather.2

commit v2 on v1

v2 whole, which is shorter than its diff:
```python
import functools
import math

import jax
import jax.numpy as jnp
import ml_dtypes
import numpy as np
from jax import lax
from jax.experimental import pallas as pl
from jax.experimental.pallas import tpu as pltpu
from jax.sharding import Mesh
from jax.sharding import PartitionSpec as P

REACH = 2
SCAN = ("z", "y", "core")
PLANE = ("z", "y")
VMEM = pl.BlockSpec(memory_space=pltpu.VMEM)
FLAG_ROWS = 8
NO_TILE = -1000
CHUNK_ROWS = 17


def moved(block, axis, distance):
    size = lax.axis_size(axis)
    return lax.ppermute(block, axis, [(i, (i + distance) % size) for i in range(size)])


def split_tables(width):
    half = width // 2
    freq, place = np.arange(half)[:, None], np.arange(half)[None, :]
    out = []
    for parity in (0, 1):
        angle = ((2 * freq + parity) * place % width) * (2.0 * np.pi / width)
        cosine, sine = np.cos(angle), np.sin(angle)
        real_form = np.block([[cosine, sine], [-sine, cosine]])
        high = real_form.astype(np.float32).astype(ml_dtypes.bfloat16)
        low = (real_form - high.astype(np.float64)).astype(np.float32).astype(ml_dtypes.bfloat16)
        out += [high, low, np.ascontiguousarray(high.T), np.ascontiguousarray(low.T)]
    return np.stack(out)


def permutation(width):
    half = width // 2
    matrix = np.zeros((width, width), np.float32)
    for parity in (0, 1):
        for index in range(half):
            matrix[2 * index + parity, parity * half + index] = 1.0
    return np.stack([matrix, matrix.T]).astype(ml_dtypes.bfloat16)


def halves(value):
    high = value.astype(jnp.bfloat16)
    return high, (value - high.astype(jnp.float32)).astype(jnp.bfloat16)


def dot(left, right):
    return jnp.dot(left, right, preferred_element_type=jnp.float32)


def table_times(high, low, field):
    field_high, field_low = halves(field)
    return dot(
        jnp.concatenate([high, high, low], axis=1),
        jnp.concatenate([field_high, field_low, field_high], axis=0),
    )


def times_table(field, high, low):
    field_high, field_low = halves(field)
    return dot(
        jnp.concatenate([field_high, field_low, field_high], axis=1),
        jnp.concatenate([high, high, low], axis=0),
    )


def rows(*blocks):
    return jnp.concatenate(blocks, axis=0)


def cols(*blocks):
    return jnp.concatenate(blocks, axis=1)


def propagated(fields, tables, kernel):
    count, width = len(fields), fields[0][0].shape[0]
    half = width // 2
    top, bottom = slice(0, half), slice(half, 2 * half)
    left, right = top, bottom
    each = [slice(i * width, (i + 1) * width) for i in range(count)]
    sums = cols(*[rows(r[top] + r[bottom], i[top] + i[bottom]) for r, i in fields])
    diffs = cols(*[rows(r[top] - r[bottom], i[top] - i[bottom]) for r, i in fields])
    bands = [table_times(tables[4 * p], tables[4 * p + 1], part) for p, part in ((0, sums), (1, diffs))]
    plus, minus = [], []
    for one in each:
        for band in bands:
            b = band[:, one]
            plus.append(cols(b[top, left] + b[top, right], b[bottom, left] + b[bottom, right]))
            minus.append(cols(b[top, left] - b[top, right], b[bottom, left] - b[bottom, right]))
    back = []
    for q, part in ((0, rows(*plus)), (1, rows(*minus))):
        freq = times_table(part, tables[4 * q + 2], tables[4 * q + 3])
        kernel_real, kernel_imag = kernel(q)
        turned = []
        for one in each:
            freq_real, freq_imag = freq[one, left], freq[one, right]
            turned.append(
                cols(
                    kernel_real * freq_real - kernel_imag * freq_imag,
                    kernel_real * freq_imag + kernel_imag * freq_real,
                )
            )
        back.append(times_table(rows(*turned), tables[4 * q], tables[4 * q + 1]))
    total, gap = back[0] + back[1], back[0] - back[1]
    out = []
    for p in (0, 1):
        stacked = []
        for i in range(count):
            band = slice(i * width + p * half, i * width + (p + 1) * half)
            stacked.append(rows(cols(total[band, left], gap[band, left]), cols(total[band, right], gap[band, right])))
        out.append(table_times(tables[4 * p + 2], tables[4 * p + 3], cols(*stacked)))
    total, gap = out[0] + out[1], out[0] - out[1]
    return [
        (rows(total[top, one], gap[top, one]), rows(total[bottom, one], gap[bottom, one])) for one in each
    ]


SIN_TERMS = [(-1.0) ** k / math.factorial(2 * k + 1) for k in range(7)]
COS_TERMS = [(-1.0) ** k / math.factorial(2 * k) for k in range(8)]


def horner(terms, square):
    total = jnp.full_like(square, terms[-1])
    for term in terms[-2::-1]:
        total = total * square + term
    return total


def cos_sin(phase):
    angle = phase * 0.5
    square = angle * angle
    sine = angle * horner(SIN_TERMS, square)
    cosine = horner(COS_TERMS, square)
    return 1.0 - 2.0 * sine * sine, 2.0 * sine * cosine


def fetched(pairs, sems):
    copies = [pltpu.make_async_copy(src, dst, sems.at[i]) for i, (src, dst) in enumerate(pairs)]
    for copy in copies:
        copy.start()
    return copies


def waited(copies):
    for copy in copies:
        copy.wait()


def slot_kernel(cover, counts, measured, own, sems):
    width = own.shape[-1]
    copies = fetched([(measured.at[0], own.at[pl.ds(0, width)])], sems)
    marker = jnp.where(counts[...] > 0, cover[...], NO_TILE).astype(jnp.float32)
    own[width:, :] = jnp.broadcast_to(marker, (FLAG_ROWS, width))
    waited(copies)


def quarter(turn, sign):
    half = turn.shape[-1] // 2

    def kernel(q):
        lanes = slice(q * half, q * half + half)
        return turn[0, :, lanes], sign * turn[1, :, lanes]

    return kernel


def forward_kernel(
    phase_in, order_in, tile_in, probe_in, tables_in, wave_out, turn_out, power_out,
    phase, order, tile, probe, tables, wave, turn, power, sems,
):
    copies = fetched(
        [(phase_in, phase), (order_in, order), (tile_in, tile), (probe_in, probe), (tables_in, tables)], sems
    )
    width = phase.shape[-1]
    scale = 1.0 / (width * width)
    waited(copies[:2])
    rest = phase[...]
    ordered = None
    for _ in range(3):
        piece = rest.astype(jnp.bfloat16)
        rest = rest - piece.astype(jnp.float32)
        piece = dot(order[1], dot(piece, order[0]).astype(jnp.bfloat16))
        ordered = piece if ordered is None else ordered + piece
    cosine, sine = cos_sin(ordered)
    turn[0] = cosine * scale
    turn[1] = sine * scale
    outs = [pltpu.make_async_copy(turn, turn_out, sems.at[5])]
    outs[0].start()
    waited(copies[2:4])
    exit_real = probe[0] * tile[0] - probe[1] * tile[1]
    exit_imag = probe[0] * tile[1] + probe[1] * tile[0]
    waited(copies[4:])
    [(real, imag)] = propagated([(exit_real, exit_imag)], [tables[i] for i in range(8)], quarter(turn, 1.0))
    power[...] = real * real + imag * imag
    for mode in range(power_out.shape[0]):
        outs.append(pltpu.make_async_copy(power, power_out.at[mode], sems.at[6 + mode]))
        outs[-1].start()
    wave[0] = real
    wave[1] = imag
    outs.append(pltpu.make_async_copy(wave, wave_out, sems.at[6 + power_out.shape[0]]))
    outs[-1].start()
    waited(outs)


def match(marker, tile_number):
    return (marker == tile_number).astype(jnp.float32)


def outbound_kernel(own_in, other_in, ahead, behind, extra, own, other, sems):
    for copy in fetched([(own_in, own), (other_in, other)], sems):
        copy.wait()
    width = own.shape[-1]
    squares = jnp.zeros((width, width), jnp.float32)
    for distance, ref in ((REACH, ahead), (-REACH, behind)):
        target = (lax.axis_index(SCAN) + distance).astype(jnp.float32)
        has_own = match(own[width : width + 1, :], target)
        has_other = match(other[width : width + 1, :], target)
        number = has_own + has_other
        share = 1.0 / jnp.maximum(number, 1.0)
        ref[:width, :] = (has_own * own[:width, :] + has_other * other[:width, :]) * share
        ref[width:, :] = jnp.broadcast_to(number, (FLAG_ROWS, width))
        gap = own[:width, :] - other[:width, :]
        squares += (0.5 * has_own * has_other) * (gap * gap)
    extra[...] = jnp.sum(squares.reshape(width // 8, 8, width), axis=0)


def main_kernel(
    extra,
    powers_in, own_in, other_in, ahead_in, behind_in, turn_in, wave_in, tables_in, tile_in, probe_in,
    chunks, terms_0, terms_1, terms_2, terms_3,
    powers, own, other, ahead, behind, turn, wave, tables, tile, probe, terms, sems,
):
    copies = fetched(
        [
            (powers_in, powers),
            (own_in, own),
            (other_in, other),
            (ahead_in, ahead),
            (behind_in, behind),
            (wave_in, wave),
            (tables_in, tables),
            (turn_in, turn),
            (tile_in, tile),
            (probe_in, probe),
        ],
        sems,
    )
    width = powers.shape[-1]
    half = width // 2
    home = lax.axis_index(SCAN).astype(jnp.float32)
    waited(copies[:5])
    modulus = jnp.sqrt((powers[0] + powers[1]) + (powers[2] + powers[3]) + 1.0)
    mismatch_sum = jnp.zeros_like(modulus)
    squares = jnp.zeros_like(modulus)
    for ref, number in (
        (own, match(own[width : width + 1, :], home)),
        (other, match(other[width : width + 1, :], home)),
        (ahead, ahead[width : width + 1, :]),
        (behind, behind[width : width + 1, :]),
    ):
        mismatch = modulus - ref[:width, :]
        scaled = number * mismatch
        mismatch_sum += scaled
        squares += scaled * mismatch
    weight = mismatch_sum / modulus
    waited(copies[5:8])
    [(real, imag)] = propagated(
        [(weight * wave[0], weight * wave[1])], [tables[i] for i in range(8)], quarter(turn, -1.0)
    )
    waited(copies[8:])
    for plane, value in enumerate((probe[0] * real + probe[1] * imag, probe[0] * imag - probe[1] * real)):
        terms[2 * plane] = value[:half]
        terms[2 * plane + 1] = value[half:]
    mode = lax.axis_index("mode")
    outs = []
    for step, out in enumerate((terms_0, terms_1, terms_2, terms_3)):
        outs.append(pltpu.make_async_copy(terms.at[lax.rem(mode + step, 4)], out, sems.at[10 + step]))
        outs[-1].start()
    loss = jnp.full((1, half), jnp.sum(squares) + jnp.sum(extra[...]))
    blocks = width // 8
    for plane, value in enumerate((tile[0] * real + tile[1] * imag, tile[0] * imag - tile[1] * real)):
        for block in range(blocks):
            lines = value[8 * block : 8 * block + 8]
            start = CHUNK_ROWS * (plane * blocks + block)
            chunks[start : start + 8, :] = lines[:, :half]
            chunks[start + 8 : start + 16, :] = lines[:, half:]
            chunks[start + 16 : start + 17, :] = loss
    waited(outs)


def object_kernel(own, one, two, three, spread):
    total = (own[...] + one[...]) + (two[...] + three[...])
    for mode in range(spread.shape[0]):
        spread[mode] = total


def finish_kernel(pieces, out):
    half = pieces.shape[1]
    for piece in range(pieces.shape[0]):
        out[0, piece // 2, half * (piece % 2) : half * (piece % 2 + 1), :] = pieces[piece]


def plane_kernel(arrived, total):
    rows_in = arrived[...]
    count = rows_in.shape[0] // CHUNK_ROWS
    parts = [rows_in[CHUNK_ROWS * i : CHUNK_ROWS * (i + 1)] for i in range(count)]
    while len(parts) > 1:
        parts = [parts[i] + parts[i + 1] for i in range(0, len(parts), 2)]
    total[: CHUNK_ROWS] = parts[0]
    total[CHUNK_ROWS:] = jnp.zeros_like(total[CHUNK_ROWS:])


def spread_kernel(one, two, spread, loss):
    total = one[...] + two[...]
    lines = cols(total[0:8], total[8:16])
    spread[...] = jnp.broadcast_to(lines[None], spread.shape)
    loss[...] = jnp.broadcast_to(total[16:17], loss.shape)


def struct(*shape):
    return jax.ShapeDtypeStruct(shape, jnp.float32)


def call(kernel, name, operands, outs, microseconds, copied=(), far=(), direct=(), sems=0, scratch=()):
    specs, placed = [], []
    anywhere = pl.BlockSpec(memory_space=pl.ANY)
    for index, operand in enumerate(operands):
        specs.append(anywhere if index in copied or index in far else VMEM)
        placed.append(pltpu.with_memory_space_constraint(operand, pltpu.HBM) if index in far else operand)
    scratch_shapes = [pltpu.VMEM(operands[i].shape, operands[i].dtype) for i in copied]
    for entry in scratch:
        buffer = outs[entry] if isinstance(entry, int) else entry
        scratch_shapes.append(pltpu.VMEM(buffer.shape, buffer.dtype))
    count = len(copied) + len(direct) + sems
    if count:
        scratch_shapes.append(pltpu.SemaphoreType.DMA((count,)))
    return pl.pallas_call(
        kernel,
        out_shape=[pltpu.HBM(o.shape, o.dtype) if i in direct else o for i, o in enumerate(outs)],
        in_specs=specs,
        out_specs=[anywhere if i in direct else VMEM for i in range(len(outs))],
        scratch_shapes=scratch_shapes,
        cost_estimate=pl.CostEstimate(
            flops=int(microseconds * 1.1e9), bytes_accessed=1 << 20, transcendentals=0
        ),
        compiler_params=pltpu.CompilerParams(vmem_limit_bytes=32 * 1024 * 1024),
        name=name,
    )(*placed)


def body(scan_size, object_tiles, probe, measured, cover, counts, phase):
    width = phase.shape[-1]
    modes = lax.axis_size("mode")
    peers = lax.axis_size(PLANE)
    tables = jnp.asarray(split_tables(width))
    order = jnp.asarray(permutation(width))
    tile, own_probe = object_tiles[0], probe[0]
    square, plane_pair = struct(width, width), struct(2, width, width)
    slot = struct(width + FLAG_ROWS, width)
    wave, turn, power = call(
        forward_kernel, "forward", (phase, order, tile, own_probe, tables),
        [plane_pair, plane_pair, struct(modes, width, width)], 4,
        copied=(0, 1, 2, 3, 4), far=(0, 1, 2, 3, 4), direct=(0, 1, 2), sems=modes - 1, scratch=(0, 1, square),
    )
    powers = lax.all_to_all(power, "mode", 0, 0, tiled=True)
    [own] = call(slot_kernel, "slot", (cover.reshape(1, 1), counts.reshape(1, 1), measured), [slot], 1, far=(2,), sems=1)
    other = moved(own, "core", 1)
    ahead, behind, extra = call(
        outbound_kernel, "outbound", (own, other), [slot, slot, struct(8, width)], 1, copied=(0, 1)
    )
    from_behind = lax.ppermute(ahead, SCAN, [(i, (i + REACH) % scan_size) for i in range(scan_size)])
    from_ahead = lax.ppermute(behind, SCAN, [(i, (i - REACH) % scan_size) for i in range(scan_size)])
    quarter_plane = struct(width // 2, width)
    chunks, *terms = call(
        main_kernel, "main",
        (extra, powers, own, other, from_behind, from_ahead, turn, wave, tables, tile, own_probe),
        [struct(peers * CHUNK_ROWS, 128)] + [quarter_plane] * modes, 4,
        copied=tuple(range(1, 11)), far=(6, 7, 8, 9, 10), direct=tuple(range(1, 1 + modes)),
        scratch=(struct(modes, width // 2, width),),
    )
    arrived = lax.all_to_all(chunks.reshape(peers, 1, CHUNK_ROWS * 128), PLANE, 0, 0, tiled=True)
    pieces = [moved(terms[step], "mode", step) for step in range(1, modes)]
    arrived, *pieces = lax.optimization_barrier((arrived, *pieces))
    [part] = call(plane_kernel, "plane", (arrived.reshape(peers * CHUNK_ROWS, 128),), [struct(24, 128)], 1)
    [object_spread] = call(
        object_kernel, "object", (terms[0], *pieces), [struct(modes, width // 2, width)], 1
    )
    spread, loss = call(
        spread_kernel, "spread", (part, moved(part, "core", 1)), [struct(peers, 8, width), struct(8, 128)], 1
    )
    probe_total = lax.all_to_all(spread, PLANE, 0, 0, tiled=True)
    [object_total] = call(
        finish_kernel, "finish", (lax.all_to_all(object_spread, "mode", 0, 0, tiled=True),),
        [struct(1, 2, width, width)], 1,
    )
    return (
        object_total,
        probe_total.reshape(1, 2, width, width),
        loss[0, 0] / (scan_size * width * width),
    )


def solution(mesh):
    scan_size, modes = mesh.shape["scan"], mesh.shape["mode"]
    cube = Mesh(mesh.devices.reshape(8, 8, 2, modes), ("z", "y", "core", "mode"))
    return jax.shard_map(
        functools.partial(body, scan_size),
        mesh=cube,
        in_specs=(
            P(SCAN, None, None, None),
            P("mode", None, None, None),
            P(SCAN, None, None),
            P(SCAN),
            P(SCAN),
            P(),
        ),
        out_specs=(P(SCAN, None, None, None), P("mode", None, None, None), P()),
        check_vma=False,
    )
```

time: 133 us -> 111 us (0.83)
  the two profiles are of different devices: /device:TPU:1 before, /device:TPU:2 now
where the time goes in v2:
time: 111 us
  starting transfers between devices  56.4 us (51%)
  waiting for transfers between devices  35.5 us (32%)
  Pallas kernels  13.6 us (12%)
  between operations  3.89 us (4%)
  local copies, waits for them, and re-layouts  1.32 us (1%)
    all_to_all x1, waiting for transfers between devices, body(): probe_total = lax.all_to_all(spread, PLANE, 0, 0, tiled=True)  15.4 us
    ppermute x5, starting transfers between devices, moved(): lax.ppermute(block, axis, [(i, (i + distance) % size) for i in range(size)])  14.3 us
    pallas_call x8, Pallas kernels, call(): pl.pallas_call(kernel, out_shape=[pltpu.HBM(o.shape, o.dtype) if i in dir...  13.6 us
    all_to_all x1, starting transfers between devices, body(): powers = lax.all_to_all(power, 'mode', 0, 0, tiled=True)  9.4 us
    ppermute x1, starting transfers between devices, body(): lax.ppermute(behind, SCAN, [(i, (i - REACH) % scan_size) for i in range(s...  9.28 us
    all_to_all x1, starting transfers between devices, body(): lax.all_to_all(chunks.reshape(peers, 1, CHUNK_ROWS * 128), PLANE, 0, 0, t...  8.76 us
    all_to_all x1, starting transfers between devices, body(): probe_total = lax.all_to_all(spread, PLANE, 0, 0, tiled=True)  7.96 us
    ppermute x5, waiting for transfers between devices, moved(): lax.ppermute(block, axis, [(i, (i + distance) % size) for i in range(size)])  5.83 us
  transfers between devices with their start and end apart: 11, of which 9 were waited for; matrix products, arithmetic and copies ran while one was open for 0% of the time, Pallas kernels for 3%

profile of v2, /device:TPU:2, one launch (start us, length us, event | category | flops | bytes accessed | tf_op | source)
XLA Modules:
  0.0 110.8 jit_solution(14201629222070062323)
XLA Ops:
  0.6 4.8 %forward.1 = (f32[2,256,256]{2,1,0:T(8,128)}, f32[2,256,256]{2,1,0:T(8,128)}, f32[4,256,256]{2,1,0:T(8,128)}) custom-call(f32[256,256]{1,0:T(8,128)} %phase_in.1, bf16[2,256,256]{2,1,0:T(8,128)(2,1)} %constant.9.clone.order_in, f32[2,256,256]{2,1,0:T(8,128)} %bitcast.12, f32[2,256,256]{2,1,0:T(8,128)} %bitcast.14, bf16[8,256,256]{2,1,0:T(8,128)(2,1)} %constant.8.clone.tables_in), custom_call_target="tpu_custom_call" | custom-call | flops 4400000000 | bytes 1048576 | tf_op jit(solution)/shard_map/forward/pallas_call | solution.py:346
  5.4 9.4 %all-to-all-start = ((f32[4,256,256]{2,1,0:T(8,128)}), f32[4,256,256]{2,1,0:T(8,128)S(1)}, u32[]{:S(2)}, u32[]{:S(2)}) async-start(f32[4,256,256]{2,1,0:T(8,128)} %get-tuple-element.21), calls=%async_computation | async-start | bytes 2097152 | tf_op jit(solution)/shard_map/all_to_all | solution.py:374
  16.1 1.0 slot.1.own_in
  17.1 1.9 %collective-permute-start = (f32[264,256]{1,0:T(8,128)S(1)}, f32[264,256]{1,0:T(8,128)S(1)}, u32[]{:S(2)}, u32[]{:S(2)}) collective-permute-start(f32[264,256]{1,0:T(8,128)S(1)} %slot.1.own_in), channel_id=1, source_target_pairs={{0,4},{4,0},{1,5},{5,1},{2,6},{6,2},{3,7},{7,3},{8,12},{12,8},{9,1... | collective-permute-start | bytes 811016 | tf_op jit(solution)/shard_map/ppermute | solution.py:25
  19.0 1.5 %collective-permute-done.other_in = f32[264,256]{1,0:T(8,128)S(1)} collective-permute-done((f32[264,256]{1,0:T(8,128)S(1)}, f32[264,256]{1,0:T(8,128)S(1)}, u32[]{:S(2)}, u32[]{:S(2)}) %collective-permute-start) | collective-permute-done | bytes 270368 | tf_op jit(solution)/shard_map/ppermute | solution.py:25
  20.5 0.2 outbound.1
  20.7 1.9 %collective-permute-start.1 = (f32[264,256]{1,0:T(8,128)S(1)}, f32[264,256]{1,0:T(8,128)S(1)}, u32[]{:S(2)}, u32[]{:S(2)}) collective-permute-start(f32[264,256]{1,0:T(8,128)S(1)} %get-tuple-element.22), channel_id=1, source_target_pairs={{0,8},{4,12},{8,16},{12,20},{16,24},{20,28},{24,32},{28,36},{32,40... | collective-permute-start | bytes 811016 | tf_op jit(solution)/shard_map/ppermute | solution.py:380
  22.7 9.3 %collective-permute-start.2 = (f32[264,256]{1,0:T(8,128)S(1)}, f32[264,256]{1,0:T(8,128)S(1)}, u32[]{:S(2)}, u32[]{:S(2)}) collective-permute-start(f32[264,256]{1,0:T(8,128)S(1)} %get-tuple-element.23), channel_id=1, source_target_pairs={{0,504},{4,508},{8,0},{12,4},{16,8},{20,12},{24,16},{28,20},{32,24... | collective-permute-start | bytes 811016 | tf_op jit(solution)/shard_map/ppermute | solution.py:381
  32.0 4.8 %collective-permute-done.1.ahead_in = f32[264,256]{1,0:T(8,128)S(1)} collective-permute-done((f32[264,256]{1,0:T(8,128)S(1)}, f32[264,256]{1,0:T(8,128)S(1)}, u32[]{:S(2)}, u32[]{:S(2)}) %collective-permute-start.1) | collective-permute-done | bytes 270368 | tf_op jit(solution)/shard_map/ppermute | solution.py:380
  36.8 1.2 %collective-permute-done.2.behind_in = f32[264,256]{1,0:T(8,128)S(1)} collective-permute-done((f32[264,256]{1,0:T(8,128)S(1)}, f32[264,256]{1,0:T(8,128)S(1)}, u32[]{:S(2)}, u32[]{:S(2)}) %collective-permute-start.2) | collective-permute-done | bytes 270368 | tf_op jit(solution)/shard_map/ppermute | solution.py:381
  38.0 0.0 all-to-all-done.powers_in
  38.0 5.1 %main.1 = (f32[1088,128]{1,0:T(8,128)}, f32[128,256]{1,0:T(8,128)}, f32[128,256]{1,0:T(8,128)}, f32[128,256]{1,0:T(8,128)}, f32[128,256]{1,0:T(8,128)}) custom-call(f32[8,256]{1,0:T(8,128)S(1)} %get-tuple-element.20.extra, f32[4,256,256]{2,1,0:T(8,128)S(1)} %all-to-all-done.powers_in, f32[264,256]{1,0:T(8,128)S(1)} %slot.1.own_in, ...), custom_call_target="tpu_custom_call" | custom-call | flops 4400000000 | bytes 1048576 | tf_op jit(solution)/shard_map/main/pallas_call | solution.py:346
  43.1 0.0 copy-start.3
  43.1 0.0 copy-start.2
  43.1 0.0 copy-start.1
  43.1 0.0 copy-start
  43.2 8.8 %all-to-all-start.1 = ((f32[64,1,2176]{2,1,0:T(1,128)}), f32[64,1,2176]{2,1,0:T(1,128)S(1)}, u32[]{:S(2)}, u32[]{:S(2)}) async-start(f32[64,1,2176]{2,1,0:T(1,128)} %bitcast.4), calls=%async_computation.1 | async-start | bytes 1114112 | tf_op jit(solution)/shard_map/all_to_all | solution.py:390
  51.9 0.0 copy-done.3
  51.9 3.4 %collective-permute-start.3 = (f32[128,256]{1,0:T(8,128)S(1)}, f32[128,256]{1,0:T(8,128)S(1)}, u32[]{:S(2)}, u32[]{:S(2)}) collective-permute-start(f32[128,256]{1,0:T(8,128)S(1)} %copy-done.3), channel_id=1, source_target_pairs={{0,1},{1,2},{2,3},{3,0},{4,5},{5,6},{6,7},{7,4},{8,9},{9,10},{10,1... | collective-permute-start | bytes 393224 | tf_op jit(solution)/shard_map/ppermute | solution.py:25
  55.3 0.0 copy-done.2
  55.3 2.5 %collective-permute-start.4 = (f32[128,256]{1,0:T(8,128)S(1)}, f32[128,256]{1,0:T(8,128)S(1)}, u32[]{:S(2)}, u32[]{:S(2)}) collective-permute-start(f32[128,256]{1,0:T(8,128)S(1)} %copy-done.2), channel_id=1, source_target_pairs={{0,2},{1,3},{2,0},{3,1},{4,6},{5,7},{6,4},{7,5},{8,10},{9,11},{10,... | collective-permute-start | bytes 393224 | tf_op jit(solution)/shard_map/ppermute | solution.py:25
  57.9 0.0 copy-done.1
  57.9 4.5 %collective-permute-start.5 = (f32[128,256]{1,0:T(8,128)S(1)}, f32[128,256]{1,0:T(8,128)S(1)}, u32[]{:S(2)}, u32[]{:S(2)}) collective-permute-start(f32[128,256]{1,0:T(8,128)S(1)} %copy-done.1), channel_id=1, source_target_pairs={{0,3},{1,0},{2,1},{3,2},{4,7},{5,4},{6,5},{7,6},{8,11},{9,8},{10,9... | collective-permute-start | bytes 393224 | tf_op jit(solution)/shard_map/ppermute | solution.py:25
  62.4 0.0 collective-permute-done.3.one
  62.4 2.1 %collective-permute-done.4.two = f32[128,256]{1,0:T(8,128)S(1)} collective-permute-done((f32[128,256]{1,0:T(8,128)S(1)}, f32[128,256]{1,0:T(8,128)S(1)}, u32[]{:S(2)}, u32[]{:S(2)}) %collective-permute-start.4) | collective-permute-done | bytes 131104 | tf_op jit(solution)/shard_map/ppermute | solution.py:25
  64.6 1.0 collective-permute-done.5.three
  65.6 5.6 %all-to-all-done.1 = f32[64,1,2176]{2,1,0:T(1,128)S(1)} async-done(((f32[64,1,2176]{2,1,0:T(1,128)}), f32[64,1,2176]{2,1,0:T(1,128)S(1)}, u32[]{:S(2)}, u32[]{:S(2)}) %all-to-all-start.1) | async-done | bytes 557088 | tf_op jit(solution)/shard_map/all_to_all | solution.py:390
  71.2 0.0 copy-done
  71.2 0.8 object.1
  72.1 4.8 %all-to-all-start.2 = ((f32[4,128,256]{2,1,0:T(8,128)}), f32[4,128,256]{2,1,0:T(8,128)S(1)}, u32[]{:S(2)}, u32[]{:S(2)}) async-start(f32[4,128,256]{2,1,0:T(8,128)} %object.1), calls=%async_computation.2 | async-start | bytes 1048576 | tf_op jit(solution)/shard_map/all_to_all | solution.py:402
  76.9 0.1 plane.1.one
  76.9 1.9 %collective-permute-start.6 = (f32[24,128]{1,0:T(8,128)S(1)}, f32[24,128]{1,0:T(8,128)S(1)}, u32[]{:S(2)}, u32[]{:S(2)}) collective-permute-start(f32[24,128]{1,0:T(8,128)S(1)} %plane.1.one), channel_id=1, source_target_pairs={{0,4},{4,0},{1,5},{5,1},{2,6},{6,2},{3,7},{7,3},{8,12},{12,8},{9,1... | collective-permute-start | bytes 36872 | tf_op jit(solution)/shard_map/ppermute | solution.py:25
  78.9 1.1 %collective-permute-done.6.two = f32[24,128]{1,0:T(8,128)S(1)} collective-permute-done((f32[24,128]{1,0:T(8,128)S(1)}, f32[24,128]{1,0:T(8,128)S(1)}, u32[]{:S(2)}, u32[]{:S(2)}) %collective-permute-start.6) | collective-permute-done | bytes 12320 | tf_op jit(solution)/shard_map/ppermute | solution.py:25
  80.0 0.8 spread.1
  80.9 2.6 %all-to-all-done.2.pieces = f32[4,128,256]{2,1,0:T(8,128)S(1)} async-done(((f32[4,128,256]{2,1,0:T(8,128)}), f32[4,128,256]{2,1,0:T(8,128)S(1)}, u32[]{:S(2)}, u32[]{:S(2)}) %all-to-all-start.2) | async-done | bytes 524320 | tf_op jit(solution)/shard_map/all_to_all | solution.py:402
  83.5 8.0 %all-to-all-start.3 = ((f32[64,8,256]{2,1,0:T(8,128)}), f32[64,8,256]{2,1,0:T(8,128)S(1)}, u32[]{:S(2)}, u32[]{:S(2)}) async-start(f32[64,8,256]{2,1,0:T(8,128)} %get-tuple-element.35), calls=%async_computation.3 | async-start | bytes 1048576 | tf_op jit(solution)/shard_map/all_to_all | solution.py:400
  91.5 0.5 slice.3
  92.6 0.8 finish.1
  93.5 15.4 %all-to-all-done.3 = f32[64,8,256]{2,1,0:T(8,128)S(1)} async-done(((f32[64,8,256]{2,1,0:T(8,128)}), f32[64,8,256]{2,1,0:T(8,128)S(1)}, u32[]{:S(2)}, u32[]{:S(2)}) %all-to-all-start.3) | async-done | bytes 524320 | tf_op jit(solution)/shard_map/all_to_all | solution.py:400
  108.8 0.8 copy.15
Async XLA Ops:
  5.4 32.6 %all-to-all-start = ((f32[4,256,256]{2,1,0:T(8,128)}), f32[4,256,256]{2,1,0:T(8,128)S(1)}, u32[]{:S(2)}, u32[]{:S(2)}) async-start(f32[4,256,256]{2,1,0:T(8,128)} %get-tuple-element.21), calls=%async_computation | async-start | bytes 2097152 | tf_op jit(solution)/shard_map/all_to_all | solution.py:374
  17.1 3.4 %collective-permute-start = (f32[264,256]{1,0:T(8,128)S(1)}, f32[264,256]{1,0:T(8,128)S(1)}, u32[]{:S(2)}, u32[]{:S(2)}) collective-permute-start(f32[264,256]{1,0:T(8,128)S(1)} %slot.1.own_in), channel_id=1, source_target_pairs={{0,4},{4,0},{1,5},{5,1},{2,6},{6,2},{3,7},{7,3},{8,12},{12,8},{9,1... | collective-permute-start | bytes 811016 | tf_op jit(solution)/shard_map/ppermute | solution.py:25
  20.7 16.1 %collective-permute-start.1 = (f32[264,256]{1,0:T(8,128)S(1)}, f32[264,256]{1,0:T(8,128)S(1)}, u32[]{:S(2)}, u32[]{:S(2)}) collective-permute-start(f32[264,256]{1,0:T(8,128)S(1)} %get-tuple-element.22), channel_id=1, source_target_pairs={{0,8},{4,12},{8,16},{12,20},{16,24},{20,28},{24,32},{28,36},{32,40... | collective-permute-start | bytes 811016 | tf_op jit(solution)/shard_map/ppermute | solution.py:380
  22.7 15.3 %collective-permute-start.2 = (f32[264,256]{1,0:T(8,128)S(1)}, f32[264,256]{1,0:T(8,128)S(1)}, u32[]{:S(2)}, u32[]{:S(2)}) collective-permute-start(f32[264,256]{1,0:T(8,128)S(1)} %get-tuple-element.23), channel_id=1, source_target_pairs={{0,504},{4,508},{8,0},{12,4},{16,8},{20,12},{24,16},{28,20},{32,24... | collective-permute-start | bytes 811016 | tf_op jit(solution)/shard_map/ppermute | solution.py:381
  43.1 8.8 %copy-start.3 = (f32[128,256]{1,0:T(8,128)S(1)}, f32[128,256]{1,0:T(8,128)}, u32[]{:S(2)}) copy-start(f32[128,256]{1,0:T(8,128)} %get-tuple-element.28) | copy-start | bytes 393220
  43.1 12.2 %copy-start.2 = (f32[128,256]{1,0:T(8,128)S(1)}, f32[128,256]{1,0:T(8,128)}, u32[]{:S(2)}) copy-start(f32[128,256]{1,0:T(8,128)} %get-tuple-element.29) | copy-start | bytes 393220
  43.1 14.7 %copy-start.1 = (f32[128,256]{1,0:T(8,128)S(1)}, f32[128,256]{1,0:T(8,128)}, u32[]{:S(2)}) copy-start(f32[128,256]{1,0:T(8,128)} %get-tuple-element.30) | copy-start | bytes 393220
  43.1 28.1 %copy-start = (f32[128,256]{1,0:T(8,128)S(1)}, f32[128,256]{1,0:T(8,128)}, u32[]{:S(2)}) copy-start(f32[128,256]{1,0:T(8,128)} %get-tuple-element.26.own) | copy-start | bytes 393220
  43.2 28.1 %all-to-all-start.1 = ((f32[64,1,2176]{2,1,0:T(1,128)}), f32[64,1,2176]{2,1,0:T(1,128)S(1)}, u32[]{:S(2)}, u32[]{:S(2)}) async-start(f32[64,1,2176]{2,1,0:T(1,128)} %bitcast.4), calls=%async_computation.1 | async-start | bytes 1114112 | tf_op jit(solution)/shard_map/all_to_all | solution.py:390
  51.9 10.5 %collective-permute-start.3 = (f32[128,256]{1,0:T(8,128)S(1)}, f32[128,256]{1,0:T(8,128)S(1)}, u32[]{:S(2)}, u32[]{:S(2)}) collective-permute-start(f32[128,256]{1,0:T(8,128)S(1)} %copy-done.3), channel_id=1, source_target_pairs={{0,1},{1,2},{2,3},{3,0},{4,5},{5,6},{6,7},{7,4},{8,9},{9,10},{10,1... | collective-permute-start | bytes 393224 | tf_op jit(solution)/shard_map/ppermute | solution.py:25
  55.3 9.2 %collective-permute-start.4 = (f32[128,256]{1,0:T(8,128)S(1)}, f32[128,256]{1,0:T(8,128)S(1)}, u32[]{:S(2)}, u32[]{:S(2)}) collective-permute-start(f32[128,256]{1,0:T(8,128)S(1)} %copy-done.2), channel_id=1, source_target_pairs={{0,2},{1,3},{2,0},{3,1},{4,6},{5,7},{6,4},{7,5},{8,10},{9,11},{10,... | collective-permute-start | bytes 393224 | tf_op jit(solution)/shard_map/ppermute | solution.py:25
  57.9 7.7 %collective-permute-start.5 = (f32[128,256]{1,0:T(8,128)S(1)}, f32[128,256]{1,0:T(8,128)S(1)}, u32[]{:S(2)}, u32[]{:S(2)}) collective-permute-start(f32[128,256]{1,0:T(8,128)S(1)} %copy-done.1), channel_id=1, source_target_pairs={{0,3},{1,0},{2,1},{3,2},{4,7},{5,4},{6,5},{7,6},{8,11},{9,8},{10,9... | collective-permute-start | bytes 393224 | tf_op jit(solution)/shard_map/ppermute | solution.py:25
  72.1 11.4 %all-to-all-start.2 = ((f32[4,128,256]{2,1,0:T(8,128)}), f32[4,128,256]{2,1,0:T(8,128)S(1)}, u32[]{:S(2)}, u32[]{:S(2)}) async-start(f32[4,128,256]{2,1,0:T(8,128)} %object.1), calls=%async_computation.2 | async-start | bytes 1048576 | tf_op jit(solution)/shard_map/all_to_all | solution.py:402
  76.9 3.1 %collective-permute-start.6 = (f32[24,128]{1,0:T(8,128)S(1)}, f32[24,128]{1,0:T(8,128)S(1)}, u32[]{:S(2)}, u32[]{:S(2)}) collective-permute-start(f32[24,128]{1,0:T(8,128)S(1)} %plane.1.one), channel_id=1, source_target_pairs={{0,4},{4,0},{1,5},{5,1},{2,6},{6,2},{3,7},{7,3},{8,12},{12,8},{9,1... | collective-permute-start | bytes 36872 | tf_op jit(solution)/shard_map/ppermute | solution.py:25
  83.5 25.4 %all-to-all-start.3 = ((f32[64,8,256]{2,1,0:T(8,128)}), f32[64,8,256]{2,1,0:T(8,128)S(1)}, u32[]{:S(2)}, u32[]{:S(2)}) async-start(f32[64,8,256]{2,1,0:T(8,128)} %get-tuple-element.35), calls=%async_computation.3 | async-start | bytes 1048576 | tf_op jit(solution)/shard_map/all_to_all | solution.py:400

commit v3 on v2

--- a/solution.py
+++ b/solution.py
@@ -15,6 +15,7 @@
 SCAN = ("z", "y", "core")
 PLANE = ("z", "y")
 VMEM = pl.BlockSpec(memory_space=pltpu.VMEM)
+SMEM = pl.BlockSpec(memory_space=pltpu.SMEM)
 FLAG_ROWS = 8
 NO_TILE = -1000
 CHUNK_ROWS = 17
@@ -155,14 +156,6 @@
         copy.wait()
 
 
-def slot_kernel(cover, counts, measured, own, sems):
-    width = own.shape[-1]
-    copies = fetched([(measured.at[0], own.at[pl.ds(0, width)])], sems)
-    marker = jnp.where(counts[...] > 0, cover[...], NO_TILE).astype(jnp.float32)
-    own[width:, :] = jnp.broadcast_to(marker, (FLAG_ROWS, width))
-    waited(copies)
-
-
 def quarter(turn, sign):
     half = turn.shape[-1] // 2
 
@@ -174,11 +167,20 @@
 
 
 def forward_kernel(
-    phase_in, order_in, tile_in, probe_in, tables_in, wave_out, turn_out, power_out,
+    phase_in, order_in, tile_in, probe_in, tables_in, cover, counts, measured,
+    own, wave_out, turn_out, power_out,
     phase, order, tile, probe, tables, wave, turn, power, sems,
 ):
     copies = fetched(
-        [(phase_in, phase), (order_in, order), (tile_in, tile), (probe_in, probe), (tables_in, tables)], sems
+        [
+            (phase_in, phase),
+            (order_in, order),
+            (tile_in, tile),
+            (probe_in, probe),
+            (tables_in, tables),
+            (measured.at[0], own.at[pl.ds(0, own.shape[1])]),
+        ],
+        sems,
     )
     width = phase.shape[-1]
     scale = 1.0 / (width * width)
@@ -193,21 +195,24 @@
     cosine, sine = cos_sin(ordered)
     turn[0] = cosine * scale
     turn[1] = sine * scale
-    outs = [pltpu.make_async_copy(turn, turn_out, sems.at[5])]
+    outs = [pltpu.make_async_copy(turn, turn_out, sems.at[6])]
     outs[0].start()
     waited(copies[2:4])
     exit_real = probe[0] * tile[0] - probe[1] * tile[1]
     exit_imag = probe[0] * tile[1] + probe[1] * tile[0]
-    waited(copies[4:])
+    waited(copies[4:5])
     [(real, imag)] = propagated([(exit_real, exit_imag)], [tables[i] for i in range(8)], quarter(turn, 1.0))
     power[...] = real * real + imag * imag
     for mode in range(power_out.shape[0]):
-        outs.append(pltpu.make_async_copy(power, power_out.at[mode], sems.at[6 + mode]))
+        outs.append(pltpu.make_async_copy(power, power_out.at[mode], sems.at[7 + mode]))
         outs[-1].start()
     wave[0] = real
     wave[1] = imag
-    outs.append(pltpu.make_async_copy(wave, wave_out, sems.at[6 + power_out.shape[0]]))
+    outs.append(pltpu.make_async_copy(wave, wave_out, sems.at[7 + power_out.shape[0]]))
     outs[-1].start()
+    waited(copies[5:])
+    marker = jnp.where(counts[0] > 0, cover[0], NO_TILE).astype(jnp.float32)
+    own[width:, :] = jnp.full((FLAG_ROWS, width), marker)
     waited(outs)
 
 
@@ -236,8 +241,8 @@
 def main_kernel(
     extra,
     powers_in, own_in, other_in, ahead_in, behind_in, turn_in, wave_in, tables_in, tile_in, probe_in,
-    chunks, terms_0, terms_1, terms_2, terms_3,
-    powers, own, other, ahead, behind, turn, wave, tables, tile, probe, terms, sems,
+    chunks_out, terms_out,
+    powers, own, other, ahead, behind, turn, wave, tables, tile, probe, chunks, terms, sems,
 ):
     copies = fetched(
         [
@@ -276,17 +281,10 @@
     [(real, imag)] = propagated(
         [(weight * wave[0], weight * wave[1])], [tables[i] for i in range(8)], quarter(turn, -1.0)
     )
-    waited(copies[8:])
-    for plane, value in enumerate((probe[0] * real + probe[1] * imag, probe[0] * imag - probe[1] * real)):
-        terms[2 * plane] = value[:half]
-        terms[2 * plane + 1] = value[half:]
-    mode = lax.axis_index("mode")
-    outs = []
-    for step, out in enumerate((terms_0, terms_1, terms_2, terms_3)):
-        outs.append(pltpu.make_async_copy(terms.at[lax.rem(mode + step, 4)], out, sems.at[10 + step]))
-        outs[-1].start()
+    waited(copies[8:9])
     loss = jnp.full((1, half), jnp.sum(squares) + jnp.sum(extra[...]))
     blocks = width // 8
+    outs = []
     for plane, value in enumerate((tile[0] * real + tile[1] * imag, tile[0] * imag - tile[1] * real)):
         for block in range(blocks):
             lines = value[8 * block : 8 * block + 8]
@@ -294,19 +292,20 @@
             chunks[start : start + 8, :] = lines[:, :half]
             chunks[start + 8 : start + 16, :] = lines[:, half:]
             chunks[start + 16 : start + 17, :] = loss
+        part = pl.ds(CHUNK_ROWS * blocks * plane, CHUNK_ROWS * blocks)
+        outs.append(pltpu.make_async_copy(chunks.at[part], chunks_out.at[part], sems.at[10 + plane]))
+        outs[-1].start()
+    waited(copies[9:])
+    terms[0] = probe[0] * real + probe[1] * imag
+    terms[1] = probe[0] * imag - probe[1] * real
+    outs.append(pltpu.make_async_copy(terms, terms_out, sems.at[12]))
+    outs[-1].start()
     waited(outs)
 
 
-def object_kernel(own, one, two, three, spread):
-    total = (own[...] + one[...]) + (two[...] + three[...])
-    for mode in range(spread.shape[0]):
-        spread[mode] = total
-
-
-def finish_kernel(pieces, out):
-    half = pieces.shape[1]
-    for piece in range(pieces.shape[0]):
-        out[0, piece // 2, half * (piece % 2) : half * (piece % 2 + 1), :] = pieces[piece]
+def object_kernel(own_in, one_in, two_in, three_in, out, own, one, two, three, sems):
+    waited(fetched([(own_in, own), (one_in, one), (two_in, two), (three_in, three)], sems))
+    out[0] = (own[...] + one[...]) + (two[...] + three[...])
 
 
 def plane_kernel(arrived, total):
@@ -334,7 +333,10 @@
     specs, placed = [], []
     anywhere = pl.BlockSpec(memory_space=pl.ANY)
     for index, operand in enumerate(operands):
-        specs.append(anywhere if index in copied or index in far else VMEM)
+        if operand.dtype == jnp.int32:
+            specs.append(SMEM)
+        else:
+            specs.append(anywhere if index in copied or index in far else VMEM)
         placed.append(pltpu.with_memory_space_constraint(operand, pltpu.HBM) if index in far else operand)
     scratch_shapes = [pltpu.VMEM(operands[i].shape, operands[i].dtype) for i in copied]
     for entry in scratch:
@@ -350,7 +352,7 @@
         out_specs=[anywhere if i in direct else VMEM for i in range(len(outs))],
         scratch_shapes=scratch_shapes,
         cost_estimate=pl.CostEstimate(
-            flops=int(microseconds * 1.1e9), bytes_accessed=1 << 20, transcendentals=0
+            flops=int(microseconds * 1.1e9), bytes_accessed=0, transcendentals=0
         ),
         compiler_params=pltpu.CompilerParams(vmem_limit_bytes=32 * 1024 * 1024),
         name=name,
@@ -366,41 +368,35 @@
     tile, own_probe = object_tiles[0], probe[0]
     square, plane_pair = struct(width, width), struct(2, width, width)
     slot = struct(width + FLAG_ROWS, width)
-    wave, turn, power = call(
-        forward_kernel, "forward", (phase, order, tile, own_probe, tables),
-        [plane_pair, plane_pair, struct(modes, width, width)], 4,
-        copied=(0, 1, 2, 3, 4), far=(0, 1, 2, 3, 4), direct=(0, 1, 2), sems=modes - 1, scratch=(0, 1, square),
+    own, wave, turn, power = call(
+        forward_kernel, "forward", (phase, order, tile, own_probe, tables, cover, counts, measured),
+        [slot, plane_pair, plane_pair, struct(modes, width, width)], 4,
+        copied=(0, 1, 2, 3, 4), far=(0, 1, 2, 3, 4, 7), direct=(1, 2, 3), sems=modes,
+        scratch=(1, 2, square),
     )
     powers = lax.all_to_all(power, "mode", 0, 0, tiled=True)
-    [own] = call(slot_kernel, "slot", (cover.reshape(1, 1), counts.reshape(1, 1), measured), [slot], 1, far=(2,), sems=1)
     other = moved(own, "core", 1)
     ahead, behind, extra = call(
         outbound_kernel, "outbound", (own, other), [slot, slot, struct(8, width)], 1, copied=(0, 1)
     )
     from_behind = lax.ppermute(ahead, SCAN, [(i, (i + REACH) % scan_size) for i in range(scan_size)])
     from_ahead = lax.ppermute(behind, SCAN, [(i, (i - REACH) % scan_size) for i in range(scan_size)])
-    quarter_plane = struct(width // 2, width)
-    chunks, *terms = call(
+    chunks, terms = call(
         main_kernel, "main",
         (extra, powers, own, other, from_behind, from_ahead, turn, wave, tables, tile, own_probe),
-        [struct(peers * CHUNK_ROWS, 128)] + [quarter_plane] * modes, 4,
-        copied=tuple(range(1, 11)), far=(6, 7, 8, 9, 10), direct=tuple(range(1, 1 + modes)),
-        scratch=(struct(modes, width // 2, width),),
+        [struct(peers * CHUNK_ROWS, 128), plane_pair], 4,
+        copied=tuple(range(1, 11)), far=(6, 7, 8, 9, 10), direct=(0, 1), sems=1, scratch=(0, 1),
     )
     arrived = lax.all_to_all(chunks.reshape(peers, 1, CHUNK_ROWS * 128), PLANE, 0, 0, tiled=True)
-    pieces = [moved(terms[step], "mode", step) for step in range(1, modes)]
-    arrived, *pieces = lax.optimization_barrier((arrived, *pieces))
-    [part] = call(plane_kernel, "plane", (arrived.reshape(peers * CHUNK_ROWS, 128),), [struct(24, 128)], 1)
-    [object_spread] = call(
-        object_kernel, "object", (terms[0], *pieces), [struct(modes, width // 2, width)], 1
-    )
+    others = [moved(terms, "mode", step) for step in (2, 1, 3)]
+    [part] = call(plane_kernel, "plane", (arrived.reshape(peers * CHUNK_ROWS, 128),), [struct(24, 128)], 0)
+    part_other = moved(part, "core", 1)
     spread, loss = call(
-        spread_kernel, "spread", (part, moved(part, "core", 1)), [struct(peers, 8, width), struct(8, 128)], 1
+        spread_kernel, "spread", (part, part_other), [struct(peers, 8, width), struct(8, 128)], 0
     )
     probe_total = lax.all_to_all(spread, PLANE, 0, 0, tiled=True)
     [object_total] = call(
-        finish_kernel, "finish", (lax.all_to_all(object_spread, "mode", 0, 0, tiled=True),),
-        [struct(1, 2, width, width)], 1,
+        object_kernel, "object", (terms, *others), [struct(1, 2, width, width)], 100, copied=(0, 1, 2, 3)
     )
     return (
         object_total,

time: 111 us -> 101 us (0.910)
  starting transfers between devices: 56.4 us -> 49.5 us
  Pallas kernels: 13.6 us -> 11.5 us
    all_to_all x1 -> x0, starting transfers between devices: 4.8 us -> none  [body(): lax.all_to_all(object_spread, 'mode', 0, 0, tiled=True)]
    ppermute x5, waiting for transfers between devices: 5.83 us -> 2.66 us  [moved(): lax.ppermute(block, axis, [(i, (i + distance) % size) for i in range(size)])]
    all_to_all x1, starting transfers between devices: 7.96 us -> 5.28 us  [body(): probe_total = lax.all_to_all(spread, PLANE, 0, 0, tiled=True)]
    all_to_all x1 -> x0, waiting for transfers between devices: 2.63 us -> none  [body(): lax.all_to_all(object_spread, 'mode', 0, 0, tiled=True)]
    all_to_all x1, waiting for transfers between devices: 5.64 us -> 8.23 us  [body(): lax.all_to_all(chunks.reshape(peers, 1, CHUNK_ROWS * 128), PLANE, 0, 0, t...]
    pallas_call x8 -> x6, Pallas kernels: 13.6 us -> 11.5 us  [call(): pl.pallas_call(kernel, out_shape=[pltpu.HBM(o.shape, o.dtype) if i in dir...]
    all_to_all x1, waiting for transfers between devices: 15.4 us -> 17.5 us  [body(): probe_total = lax.all_to_all(spread, PLANE, 0, 0, tiled=True)]
  transfers between devices with their start and end apart: 11 -> 10, of which waited for: 9 -> 6; matrix products, arithmetic and copies ran while one was open for 0% -> 1% of each run, Pallas kernels for 3% -> 2%
where the time goes in v3:
time: 101 us
  starting transfers between devices  49.5 us (49%)
  waiting for transfers between devices  34.4 us (34%)
  Pallas kernels  11.5 us (11%)
  between operations  3.85 us (4%)
  local copies, waits for them, and re-layouts  1.31 us (1%)
    all_to_all x1, waiting for transfers between devices, body(): probe_total = lax.all_to_all(spread, PLANE, 0, 0, tiled=True)  17.5 us
    ppermute x5, starting transfers between devices, moved(): lax.ppermute(block, axis, [(i, (i + distance) % size) for i in range(size)])  14.9 us
    pallas_call x6, Pallas kernels, call(): pl.pallas_call(kernel, out_shape=[pltpu.HBM(o.shape, o.dtype) if i in dir...  11.5 us
    all_to_all x1, starting transfers between devices, body(): powers = lax.all_to_all(power, 'mode', 0, 0, tiled=True)  9.4 us
    ppermute x1, starting transfers between devices, body(): lax.ppermute(behind, SCAN, [(i, (i - REACH) % scan_size) for i in range(s...  9.29 us
    all_to_all x1, starting transfers between devices, body(): lax.all_to_all(chunks.reshape(peers, 1, CHUNK_ROWS * 128), PLANE, 0, 0, t...  8.75 us
    all_to_all x1, waiting for transfers between devices, body(): lax.all_to_all(chunks.reshape(peers, 1, CHUNK_ROWS * 128), PLANE, 0, 0, t...  8.23 us
    all_to_all x1, starting transfers between devices, body(): probe_total = lax.all_to_all(spread, PLANE, 0, 0, tiled=True)  5.28 us
  transfers between devices with their start and end apart: 10, of which 6 were waited for; matrix products, arithmetic and copies ran while one was open for 1% of the time, Pallas kernels for 2%

profile of v3, /device:TPU:2, one launch (start us, length us, event | category | flops | bytes accessed | tf_op | source)
XLA Modules:
  0.0 100.5 jit_solution(14850265459413883916)
XLA Ops:
  1.9 4.8 %forward.1 = (f32[264,256]{1,0:T(8,128)S(1)}, f32[2,256,256]{2,1,0:T(8,128)}, f32[2,256,256]{2,1,0:T(8,128)}, f32[4,256,256]{2,1,0:T(8,128)}) custom-call(f32[256,256]{1,0:T(8,128)} %phase_in.1, bf16[2,256,256]{2,1,0:T(8,128)(2,1)} %constant.9.clone.order_in, f32[2,256,256]{2,1,0:T(8,128)} %bitcast.9, f32[2,256,256]{2,1,0:T(8,128)} %bitcast.11, ...), custom_call_target="tpu_custom_call" | custom-call | flops 4400000000 | tf_op jit(solution)/shard_map/forward/pallas_call | solution.py:348
  6.7 9.4 %all-to-all-start = ((f32[4,256,256]{2,1,0:T(8,128)}), f32[4,256,256]{2,1,0:T(8,128)S(1)}, u32[]{:S(2)}, u32[]{:S(2)}) async-start(f32[4,256,256]{2,1,0:T(8,128)} %get-tuple-element.16), calls=%async_computation | async-start | bytes 2097152 | tf_op jit(solution)/shard_map/all_to_all | solution.py:377
  16.1 1.9 %collective-permute-start = (f32[264,256]{1,0:T(8,128)S(1)}, f32[264,256]{1,0:T(8,128)S(1)}, u32[]{:S(2)}, u32[]{:S(2)}) collective-permute-start(f32[264,256]{1,0:T(8,128)S(1)} %get-tuple-element.14.own_in), channel_id=1, source_target_pairs={{0,4},{4,0},{1,5},{5,1},{2,6},{6,2},{3,7},{7,3},{8,12},{12,8},{9,1... | collective-permute-start | bytes 811016 | tf_op jit(solution)/shard_map/ppermute | solution.py:26
  18.0 1.5 %collective-permute-done.other_in = f32[264,256]{1,0:T(8,128)S(1)} collective-permute-done((f32[264,256]{1,0:T(8,128)S(1)}, f32[264,256]{1,0:T(8,128)S(1)}, u32[]{:S(2)}, u32[]{:S(2)}) %collective-permute-start) | collective-permute-done | bytes 270368 | tf_op jit(solution)/shard_map/ppermute | solution.py:26
  19.5 0.2 outbound.1
  19.8 1.9 %collective-permute-start.1 = (f32[264,256]{1,0:T(8,128)S(1)}, f32[264,256]{1,0:T(8,128)S(1)}, u32[]{:S(2)}, u32[]{:S(2)}) collective-permute-start(f32[264,256]{1,0:T(8,128)S(1)} %get-tuple-element.17), channel_id=1, source_target_pairs={{0,8},{4,12},{8,16},{12,20},{16,24},{20,28},{24,32},{28,36},{32,40... | collective-permute-start | bytes 811016 | tf_op jit(solution)/shard_map/ppermute | solution.py:382
  21.7 9.3 %collective-permute-start.2 = (f32[264,256]{1,0:T(8,128)S(1)}, f32[264,256]{1,0:T(8,128)S(1)}, u32[]{:S(2)}, u32[]{:S(2)}) collective-permute-start(f32[264,256]{1,0:T(8,128)S(1)} %get-tuple-element.18), channel_id=1, source_target_pairs={{0,504},{4,508},{8,0},{12,4},{16,8},{20,12},{24,16},{28,20},{32,24... | collective-permute-start | bytes 811016 | tf_op jit(solution)/shard_map/ppermute | solution.py:383
  31.0 4.8 %collective-permute-done.1.ahead_in = f32[264,256]{1,0:T(8,128)S(1)} collective-permute-done((f32[264,256]{1,0:T(8,128)S(1)}, f32[264,256]{1,0:T(8,128)S(1)}, u32[]{:S(2)}, u32[]{:S(2)}) %collective-permute-start.1) | collective-permute-done | bytes 270368 | tf_op jit(solution)/shard_map/ppermute | solution.py:382
  35.8 1.2 %collective-permute-done.2.behind_in = f32[264,256]{1,0:T(8,128)S(1)} collective-permute-done((f32[264,256]{1,0:T(8,128)S(1)}, f32[264,256]{1,0:T(8,128)S(1)}, u32[]{:S(2)}, u32[]{:S(2)}) %collective-permute-start.2) | collective-permute-done | bytes 270368 | tf_op jit(solution)/shard_map/ppermute | solution.py:383
  37.0 0.0 all-to-all-done.powers_in
  37.0 4.5 %main.1 = (f32[1088,128]{1,0:T(8,128)}, f32[2,256,256]{2,1,0:T(8,128)}) custom-call(f32[8,256]{1,0:T(8,128)S(1)} %get-tuple-element.15.extra, f32[4,256,256]{2,1,0:T(8,128)S(1)} %all-to-all-done.powers_in, f32[264,256]{1,0:T(8,128)S(1)} %get-tuple-element.14.own_in, f32[264,256]{1,0:T(8,128)S(1)} %collective-permute-done.other_in, ...), custom_call_target="tpu_custom_call" | custom-call | flops 4400000000 | tf_op jit(solution)/shard_map/main/pallas_call | solution.py:348
  41.5 0.0 copy-start
  41.5 8.7 %all-to-all-start.1 = ((f32[64,1,2176]{2,1,0:T(1,128)}), f32[64,1,2176]{2,1,0:T(1,128)S(1)}, u32[]{:S(2)}, u32[]{:S(2)}) async-start(f32[64,1,2176]{2,1,0:T(1,128)} %bitcast.8), calls=%async_computation.1 | async-start | bytes 1114112 | tf_op jit(solution)/shard_map/all_to_all | solution.py:390
  50.3 0.0 copy-done
  50.3 1.9 %collective-permute-start.5 = (f32[2,256,256]{2,1,0:T(8,128)S(1)}, f32[2,256,256]{2,1,0:T(8,128)S(1)}, u32[]{:S(2)}, u32[]{:S(2)}) collective-permute-start(f32[2,256,256]{2,1,0:T(8,128)S(1)} %copy-done), channel_id=1, source_target_pairs={{0,3},{1,0},{2,1},{3,2},{4,7},{5,4},{6,5},{7,6},{8,11},{9,8},{10,9... | collective-permute-start | bytes 1572872 | tf_op jit(solution)/shard_map/ppermute | solution.py:26
  52.2 3.9 %collective-permute-start.4 = (f32[2,256,256]{2,1,0:T(8,128)S(1)}, f32[2,256,256]{2,1,0:T(8,128)S(1)}, u32[]{:S(2)}, u32[]{:S(2)}) collective-permute-start(f32[2,256,256]{2,1,0:T(8,128)S(1)} %copy-done), channel_id=1, source_target_pairs={{0,1},{1,2},{2,3},{3,0},{4,5},{5,6},{6,7},{7,4},{8,9},{9,10},{10,1... | collective-permute-start | bytes 1572872 | tf_op jit(solution)/shard_map/ppermute | solution.py:26
  56.1 5.2 %collective-permute-start.3 = (f32[2,256,256]{2,1,0:T(8,128)S(1)}, f32[2,256,256]{2,1,0:T(8,128)S(1)}, u32[]{:S(2)}, u32[]{:S(2)}) collective-permute-start(f32[2,256,256]{2,1,0:T(8,128)S(1)} %copy-done), channel_id=1, source_target_pairs={{0,2},{1,3},{2,0},{3,1},{4,6},{5,7},{6,4},{7,5},{8,10},{9,11},{10,... | collective-permute-start | bytes 1572872 | tf_op jit(solution)/shard_map/ppermute | solution.py:26
  61.3 8.2 %all-to-all-done.1 = f32[64,1,2176]{2,1,0:T(1,128)S(1)} async-done(((f32[64,1,2176]{2,1,0:T(1,128)}), f32[64,1,2176]{2,1,0:T(1,128)S(1)}, u32[]{:S(2)}, u32[]{:S(2)}) %all-to-all-start.1) | async-done | bytes 557088 | tf_op jit(solution)/shard_map/all_to_all | solution.py:390
  69.6 0.1 plane.1.one
  69.6 1.9 %collective-permute-start.6 = (f32[24,128]{1,0:T(8,128)S(1)}, f32[24,128]{1,0:T(8,128)S(1)}, u32[]{:S(2)}, u32[]{:S(2)}) collective-permute-start(f32[24,128]{1,0:T(8,128)S(1)} %plane.1.one), channel_id=1, source_target_pairs={{0,4},{4,0},{1,5},{5,1},{2,6},{6,2},{3,7},{7,3},{8,12},{12,8},{9,1... | collective-permute-start | bytes 36872 | tf_op jit(solution)/shard_map/ppermute | solution.py:26
  71.6 1.1 %collective-permute-done.6.two = f32[24,128]{1,0:T(8,128)S(1)} collective-permute-done((f32[24,128]{1,0:T(8,128)S(1)}, f32[24,128]{1,0:T(8,128)S(1)}, u32[]{:S(2)}, u32[]{:S(2)}) %collective-permute-start.6) | collective-permute-done | bytes 12320 | tf_op jit(solution)/shard_map/ppermute | solution.py:26
  72.7 0.8 spread.1
  73.5 5.3 %all-to-all-start.2 = ((f32[64,8,256]{2,1,0:T(8,128)}), f32[64,8,256]{2,1,0:T(8,128)S(1)}, u32[]{:S(2)}, u32[]{:S(2)}) async-start(f32[64,8,256]{2,1,0:T(8,128)} %get-tuple-element.23), calls=%async_computation.2 | async-start | bytes 1048576 | tf_op jit(solution)/shard_map/all_to_all | solution.py:397
  78.8 0.0 collective-permute-done.5.three_in
  78.8 0.0 collective-permute-done.4.two_in
  78.9 0.0 collective-permute-done.3.one_in
  78.9 1.1 %object.1 = f32[1,2,256,256]{3,2,1,0:T(8,128)} custom-call(f32[2,256,256]{2,1,0:T(8,128)S(1)} %copy-done, f32[2,256,256]{2,1,0:T(8,128)S(1)} %collective-permute-done.3.one_in, f32[2,256,256]{2,1,0:T(8,128)S(1)} %collective-permute-done.4.two_in, f32[2,256,256]{2,1,0:T(8,128)S(1)} %collective-permute-done.5.three_in), custom_call_target="tpu_custom_call" | custom-call | flops 109999996928 | tf_op jit(solution)/shard_map/object/pallas_call | solution.py:348
  80.0 0.5 slice.3
  81.1 17.5 %all-to-all-done.2 = f32[64,8,256]{2,1,0:T(8,128)S(1)} async-done(((f32[64,8,256]{2,1,0:T(8,128)}), f32[64,8,256]{2,1,0:T(8,128)S(1)}, u32[]{:S(2)}, u32[]{:S(2)}) %all-to-all-start.2) | async-done | bytes 524320 | tf_op jit(solution)/shard_map/all_to_all | solution.py:397
  98.6 0.8 copy.15
Async XLA Ops:
  6.7 30.3 %all-to-all-start = ((f32[4,256,256]{2,1,0:T(8,128)}), f32[4,256,256]{2,1,0:T(8,128)S(1)}, u32[]{:S(2)}, u32[]{:S(2)}) async-start(f32[4,256,256]{2,1,0:T(8,128)} %get-tuple-element.16), calls=%async_computation | async-start | bytes 2097152 | tf_op jit(solution)/shard_map/all_to_all | solution.py:377
  16.1 3.4 %collective-permute-start = (f32[264,256]{1,0:T(8,128)S(1)}, f32[264,256]{1,0:T(8,128)S(1)}, u32[]{:S(2)}, u32[]{:S(2)}) collective-permute-start(f32[264,256]{1,0:T(8,128)S(1)} %get-tuple-element.14.own_in), channel_id=1, source_target_pairs={{0,4},{4,0},{1,5},{5,1},{2,6},{6,2},{3,7},{7,3},{8,12},{12,8},{9,1... | collective-permute-start | bytes 811016 | tf_op jit(solution)/shard_map/ppermute | solution.py:26
  19.8 16.1 %collective-permute-start.1 = (f32[264,256]{1,0:T(8,128)S(1)}, f32[264,256]{1,0:T(8,128)S(1)}, u32[]{:S(2)}, u32[]{:S(2)}) collective-permute-start(f32[264,256]{1,0:T(8,128)S(1)} %get-tuple-element.17), channel_id=1, source_target_pairs={{0,8},{4,12},{8,16},{12,20},{16,24},{20,28},{24,32},{28,36},{32,40... | collective-permute-start | bytes 811016 | tf_op jit(solution)/shard_map/ppermute | solution.py:382
  21.7 15.3 %collective-permute-start.2 = (f32[264,256]{1,0:T(8,128)S(1)}, f32[264,256]{1,0:T(8,128)S(1)}, u32[]{:S(2)}, u32[]{:S(2)}) collective-permute-start(f32[264,256]{1,0:T(8,128)S(1)} %get-tuple-element.18), channel_id=1, source_target_pairs={{0,504},{4,508},{8,0},{12,4},{16,8},{20,12},{24,16},{28,20},{32,24... | collective-permute-start | bytes 811016 | tf_op jit(solution)/shard_map/ppermute | solution.py:383
  41.5 8.8 %copy-start = (f32[2,256,256]{2,1,0:T(8,128)S(1)}, f32[2,256,256]{2,1,0:T(8,128)}, u32[]{:S(2)}) copy-start(f32[2,256,256]{2,1,0:T(8,128)} %get-tuple-element.21.own_in) | copy-start | bytes 1572868
  41.5 28.1 %all-to-all-start.1 = ((f32[64,1,2176]{2,1,0:T(1,128)}), f32[64,1,2176]{2,1,0:T(1,128)S(1)}, u32[]{:S(2)}, u32[]{:S(2)}) async-start(f32[64,1,2176]{2,1,0:T(1,128)} %bitcast.8), calls=%async_computation.1 | async-start | bytes 1114112 | tf_op jit(solution)/shard_map/all_to_all | solution.py:390
  50.3 28.6 %collective-permute-start.5 = (f32[2,256,256]{2,1,0:T(8,128)S(1)}, f32[2,256,256]{2,1,0:T(8,128)S(1)}, u32[]{:S(2)}, u32[]{:S(2)}) collective-permute-start(f32[2,256,256]{2,1,0:T(8,128)S(1)} %copy-done), channel_id=1, source_target_pairs={{0,3},{1,0},{2,1},{3,2},{4,7},{5,4},{6,5},{7,6},{8,11},{9,8},{10,9... | collective-permute-start | bytes 1572872 | tf_op jit(solution)/shard_map/ppermute | solution.py:26
  52.2 26.6 %collective-permute-start.4 = (f32[2,256,256]{2,1,0:T(8,128)S(1)}, f32[2,256,256]{2,1,0:T(8,128)S(1)}, u32[]{:S(2)}, u32[]{:S(2)}) collective-permute-start(f32[2,256,256]{2,1,0:T(8,128)S(1)} %copy-done), channel_id=1, source_target_pairs={{0,1},{1,2},{2,3},{3,0},{4,5},{5,6},{6,7},{7,4},{8,9},{9,10},{10,1... | collective-permute-start | bytes 1572872 | tf_op jit(solution)/shard_map/ppermute | solution.py:26
  56.1 22.7 %collective-permute-start.3 = (f32[2,256,256]{2,1,0:T(8,128)S(1)}, f32[2,256,256]{2,1,0:T(8,128)S(1)}, u32[]{:S(2)}, u32[]{:S(2)}) collective-permute-start(f32[2,256,256]{2,1,0:T(8,128)S(1)} %copy-done), channel_id=1, source_target_pairs={{0,2},{1,3},{2,0},{3,1},{4,6},{5,7},{6,4},{7,5},{8,10},{9,11},{10,... | collective-permute-start | bytes 1572872 | tf_op jit(solution)/shard_map/ppermute | solution.py:26
  69.6 3.1 %collective-permute-start.6 = (f32[24,128]{1,0:T(8,128)S(1)}, f32[24,128]{1,0:T(8,128)S(1)}, u32[]{:S(2)}, u32[]{:S(2)}) collective-permute-start(f32[24,128]{1,0:T(8,128)S(1)} %plane.1.one), channel_id=1, source_target_pairs={{0,4},{4,0},{1,5},{5,1},{2,6},{6,2},{3,7},{7,3},{8,12},{12,8},{9,1... | collective-permute-start | bytes 36872 | tf_op jit(solution)/shard_map/ppermute | solution.py:26
  73.5 25.0 %all-to-all-start.2 = ((f32[64,8,256]{2,1,0:T(8,128)}), f32[64,8,256]{2,1,0:T(8,128)S(1)}, u32[]{:S(2)}, u32[]{:S(2)}) async-start(f32[64,8,256]{2,1,0:T(8,128)} %get-tuple-element.23), calls=%async_computation.2 | async-start | bytes 1048576 | tf_op jit(solution)/shard_map/all_to_all | solution.py:397

commit v4 on v3

--- a/solution.py
+++ b/solution.py
@@ -11,7 +11,6 @@
 from jax.sharding import Mesh
 from jax.sharding import PartitionSpec as P
 
-REACH = 2
 SCAN = ("z", "y", "core")
 PLANE = ("z", "y")
 VMEM = pl.BlockSpec(memory_space=pltpu.VMEM)
@@ -36,8 +35,8 @@
         real_form = np.block([[cosine, sine], [-sine, cosine]])
         high = real_form.astype(np.float32).astype(ml_dtypes.bfloat16)
         low = (real_form - high.astype(np.float64)).astype(np.float32).astype(ml_dtypes.bfloat16)
-        out += [high, low, np.ascontiguousarray(high.T), np.ascontiguousarray(low.T)]
-    return np.stack(out)
+        out += [high, low]
+    return np.stack(out + [np.ascontiguousarray(table.T) for table in out])
 
 
 def permutation(width):
@@ -46,7 +45,7 @@
     for parity in (0, 1):
         for index in range(half):
             matrix[2 * index + parity, parity * half + index] = 1.0
-    return np.stack([matrix, matrix.T]).astype(ml_dtypes.bfloat16)
+    return matrix.astype(ml_dtypes.bfloat16)
 
 
 def halves(value):
@@ -82,7 +81,12 @@
     return jnp.concatenate(blocks, axis=1)
 
 
-def propagated(fields, tables, kernel):
+def waited(copies):
+    for copy in copies:
+        copy.wait()
+
+
+def propagated(fields, tables, kernel, second=(), third=()):
     count, width = len(fields), fields[0][0].shape[0]
     half = width // 2
     top, bottom = slice(0, half), slice(half, 2 * half)
@@ -90,7 +94,7 @@
     each = [slice(i * width, (i + 1) * width) for i in range(count)]
     sums = cols(*[rows(r[top] + r[bottom], i[top] + i[bottom]) for r, i in fields])
     diffs = cols(*[rows(r[top] - r[bottom], i[top] - i[bottom]) for r, i in fields])
-    bands = [table_times(tables[4 * p], tables[4 * p + 1], part) for p, part in ((0, sums), (1, diffs))]
+    bands = [table_times(tables[2 * p], tables[2 * p + 1], part) for p, part in ((0, sums), (1, diffs))]
     plus, minus = [], []
     for one in each:
         for band in bands:
@@ -98,8 +102,12 @@
             plus.append(cols(b[top, left] + b[top, right], b[bottom, left] + b[bottom, right]))
             minus.append(cols(b[top, left] - b[top, right], b[bottom, left] - b[bottom, right]))
     back = []
-    for q, part in ((0, rows(*plus)), (1, rows(*minus))):
-        freq = times_table(part, tables[4 * q + 2], tables[4 * q + 3])
+    waited(second)
+    freqs = [
+        times_table(rows(*part), tables[2 * q + 4], tables[2 * q + 5]) for q, part in ((0, plus), (1, minus))
+    ]
+    waited(third)
+    for q, freq in enumerate(freqs):
         kernel_real, kernel_imag = kernel(q)
         turned = []
         for one in each:
@@ -110,7 +118,7 @@
                     kernel_real * freq_imag + kernel_imag * freq_real,
                 )
             )
-        back.append(times_table(rows(*turned), tables[4 * q], tables[4 * q + 1]))
+        back.append(times_table(rows(*turned), tables[2 * q], tables[2 * q + 1]))
     total, gap = back[0] + back[1], back[0] - back[1]
     out = []
     for p in (0, 1):
@@ -118,7 +126,7 @@
         for i in range(count):
             band = slice(i * width + p * half, i * width + (p + 1) * half)
             stacked.append(rows(cols(total[band, left], gap[band, left]), cols(total[band, right], gap[band, right])))
-        out.append(table_times(tables[4 * p + 2], tables[4 * p + 3], cols(*stacked)))
+        out.append(table_times(tables[2 * p + 4], tables[2 * p + 5], cols(*stacked)))
     total, gap = out[0] + out[1], out[0] - out[1]
     return [
         (rows(total[top, one], gap[top, one]), rows(total[bottom, one], gap[bottom, one])) for one in each
@@ -151,11 +159,6 @@
     return copies
 
 
-def waited(copies):
-    for copy in copies:
-        copy.wait()
-
-
 def quarter(turn, sign):
     half = turn.shape[-1] // 2
 
@@ -169,48 +172,52 @@
 def forward_kernel(
     phase_in, order_in, tile_in, probe_in, tables_in, cover, counts, measured,
     own, wave_out, turn_out, power_out,
-    phase, order, tile, probe, tables, wave, turn, power, sems,
+    order, tile, probe, tables, phase, wave, turn, power, sems,
 ):
+    width = phase_in.shape[-1]
+    half = width // 2
     copies = fetched(
         [
-            (phase_in, phase),
+            (phase_in.at[:, pl.ds(0, half)], phase.at[0]),
+            (phase_in.at[:, pl.ds(half, half)], phase.at[1]),
             (order_in, order),
             (tile_in, tile),
             (probe_in, probe),
-            (tables_in, tables),
+            (tables_in.at[pl.ds(0, 4)], tables.at[pl.ds(0, 4)]),
+            (tables_in.at[pl.ds(4, 4)], tables.at[pl.ds(4, 4)]),
             (measured.at[0], own.at[pl.ds(0, own.shape[1])]),
         ],
         sems,
     )
-    width = phase.shape[-1]
     scale = 1.0 / (width * width)
-    waited(copies[:2])
-    rest = phase[...]
+    waited(copies[:3])
+    swap = order[...]
+    rest = rows(*[cols(*[phase[h, pl.ds(p, half, stride=2), :] for h in (0, 1)]) for p in (0, 1)])
     ordered = None
     for _ in range(3):
         piece = rest.astype(jnp.bfloat16)
         rest = rest - piece.astype(jnp.float32)
-        piece = dot(order[1], dot(piece, order[0]).astype(jnp.bfloat16))
+        piece = dot(piece, swap)
         ordered = piece if ordered is None else ordered + piece
     cosine, sine = cos_sin(ordered)
     turn[0] = cosine * scale
     turn[1] = sine * scale
-    outs = [pltpu.make_async_copy(turn, turn_out, sems.at[6])]
+    outs = [pltpu.make_async_copy(turn, turn_out, sems.at[8])]
     outs[0].start()
-    waited(copies[2:4])
+    waited(copies[3:5])
     exit_real = probe[0] * tile[0] - probe[1] * tile[1]
     exit_imag = probe[0] * tile[1] + probe[1] * tile[0]
-    waited(copies[4:5])
-    [(real, imag)] = propagated([(exit_real, exit_imag)], [tables[i] for i in range(8)], quarter(turn, 1.0))
+    waited(copies[5:6])
+    [(real, imag)] = propagated([(exit_real, exit_imag)], tables, quarter(turn, 1.0), second=copies[6:7])
     power[...] = real * real + imag * imag
     for mode in range(power_out.shape[0]):
-        outs.append(pltpu.make_async_copy(power, power_out.at[mode], sems.at[7 + mode]))
+        outs.append(pltpu.make_async_copy(power, power_out.at[mode], sems.at[9 + mode]))
         outs[-1].start()
     wave[0] = real
     wave[1] = imag
-    outs.append(pltpu.make_async_copy(wave, wave_out, sems.at[7 + power_out.shape[0]]))
+    outs.append(pltpu.make_async_copy(wave, wave_out, sems.at[9 + power_out.shape[0]]))
     outs[-1].start()
-    waited(copies[5:])
+    waited(copies[7:])
     marker = jnp.where(counts[0] > 0, cover[0], NO_TILE).astype(jnp.float32)
     own[width:, :] = jnp.full((FLAG_ROWS, width), marker)
     waited(outs)
@@ -220,39 +227,32 @@
     return (marker == tile_number).astype(jnp.float32)
 
 
-def outbound_kernel(own_in, other_in, ahead, behind, extra, own, other, sems):
-    for copy in fetched([(own_in, own), (other_in, other)], sems):
-        copy.wait()
+def partner_kernel(own, across, combined, extra):
     width = own.shape[-1]
-    squares = jnp.zeros((width, width), jnp.float32)
-    for distance, ref in ((REACH, ahead), (-REACH, behind)):
-        target = (lax.axis_index(SCAN) + distance).astype(jnp.float32)
-        has_own = match(own[width : width + 1, :], target)
-        has_other = match(other[width : width + 1, :], target)
-        number = has_own + has_other
-        share = 1.0 / jnp.maximum(number, 1.0)
-        ref[:width, :] = (has_own * own[:width, :] + has_other * other[:width, :]) * share
-        ref[width:, :] = jnp.broadcast_to(number, (FLAG_ROWS, width))
-        gap = own[:width, :] - other[:width, :]
-        squares += (0.5 * has_own * has_other) * (gap * gap)
+    core = lax.axis_index("core")
+    target = (lax.axis_index(SCAN) + 1 - 2 * core).astype(jnp.float32)
+    has_own = match(own[width : width + 1, :], target)
+    has_across = match(across[width : width + 1, :], target)
+    number = has_own + has_across
+    share = 1.0 / jnp.maximum(number, 1.0)
+    combined[:width, :] = (has_own * own[:width, :] + has_across * across[:width, :]) * share
+    combined[width:, :] = jnp.broadcast_to(number, (FLAG_ROWS, width))
+    gap = own[:width, :] - across[:width, :]
+    squares = (0.5 * has_own * has_across) * (gap * gap)
     extra[...] = jnp.sum(squares.reshape(width // 8, 8, width), axis=0)
 
 
 def main_kernel(
-    extra,
-    powers_in, own_in, other_in, ahead_in, behind_in, turn_in, wave_in, tables_in, tile_in, probe_in,
-    chunks_out, terms_out,
-    powers, own, other, ahead, behind, turn, wave, tables, tile, probe, chunks, terms, sems,
+    extra, powers, own, across, beyond, partner,
+    turn_in, wave_in, tables_in, tile_in, probe_in,
+    chunks_out, terms,
+    turn, wave, tables, tile, probe, chunks, sems,
 ):
     copies = fetched(
         [
-            (powers_in, powers),
-            (own_in, own),
-            (other_in, other),
-            (ahead_in, ahead),
-            (behind_in, behind),
             (wave_in, wave),
-            (tables_in, tables),
+            (tables_in.at[pl.ds(0, 4)], tables.at[pl.ds(0, 4)]),
+            (tables_in.at[pl.ds(4, 4)], tables.at[pl.ds(4, 4)]),
             (turn_in, turn),
             (tile_in, tile),
             (probe_in, probe),
@@ -262,26 +262,25 @@
     width = powers.shape[-1]
     half = width // 2
     home = lax.axis_index(SCAN).astype(jnp.float32)
-    waited(copies[:5])
     modulus = jnp.sqrt((powers[0] + powers[1]) + (powers[2] + powers[3]) + 1.0)
     mismatch_sum = jnp.zeros_like(modulus)
     squares = jnp.zeros_like(modulus)
     for ref, number in (
         (own, match(own[width : width + 1, :], home)),
-        (other, match(other[width : width + 1, :], home)),
-        (ahead, ahead[width : width + 1, :]),
-        (behind, behind[width : width + 1, :]),
+        (across, match(across[width : width + 1, :], home)),
+        (beyond, match(beyond[width : width + 1, :], home)),
+        (partner, partner[width : width + 1, :]),
     ):
         mismatch = modulus - ref[:width, :]
         scaled = number * mismatch
         mismatch_sum += scaled
         squares += scaled * mismatch
     weight = mismatch_sum / modulus
-    waited(copies[5:8])
+    waited(copies[:2])
     [(real, imag)] = propagated(
-        [(weight * wave[0], weight * wave[1])], [tables[i] for i in range(8)], quarter(turn, -1.0)
-    )
-    waited(copies[8:9])
+        [(weight * wave[0], weight * wave[1])], tables, quarter(turn, -1.0), copies[2:3], copies[3:4]
+    )
+    waited(copies[4:])
     loss = jnp.full((1, half), jnp.sum(squares) + jnp.sum(extra[...]))
     blocks = width // 8
     outs = []
@@ -293,13 +292,10 @@
             chunks[start + 8 : start + 16, :] = lines[:, half:]
             chunks[start + 16 : start + 17, :] = loss
         part = pl.ds(CHUNK_ROWS * blocks * plane, CHUNK_ROWS * blocks)
-        outs.append(pltpu.make_async_copy(chunks.at[part], chunks_out.at[part], sems.at[10 + plane]))
+        outs.append(pltpu.make_async_copy(chunks.at[part], chunks_out.at[part], sems.at[6 + plane]))
         outs[-1].start()
-    waited(copies[9:])
     terms[0] = probe[0] * real + probe[1] * imag
     terms[1] = probe[0] * imag - probe[1] * real
-    outs.append(pltpu.make_async_copy(terms, terms_out, sems.at[12]))
-    outs[-1].start()
     waited(outs)
 
 
@@ -318,11 +314,15 @@
     total[CHUNK_ROWS:] = jnp.zeros_like(total[CHUNK_ROWS:])
 
 
-def spread_kernel(one, two, spread, loss):
+def spread_kernel(one, two, spread, loss, block, sems):
     total = one[...] + two[...]
     lines = cols(total[0:8], total[8:16])
-    spread[...] = jnp.broadcast_to(lines[None], spread.shape)
+    count = block.shape[0]
+    block[...] = jnp.broadcast_to(lines[None], block.shape)
+    parts = [pl.ds(i, count) for i in range(0, spread.shape[0], count)]
+    copies = fetched([(block, spread.at[part]) for part in parts], sems)
     loss[...] = jnp.broadcast_to(total[16:17], loss.shape)
+    waited(copies)
 
 
 def struct(*shape):
@@ -371,28 +371,30 @@
     own, wave, turn, power = call(
         forward_kernel, "forward", (phase, order, tile, own_probe, tables, cover, counts, measured),
         [slot, plane_pair, plane_pair, struct(modes, width, width)], 4,
-        copied=(0, 1, 2, 3, 4), far=(0, 1, 2, 3, 4, 7), direct=(1, 2, 3), sems=modes,
-        scratch=(1, 2, square),
+        copied=(1, 2, 3, 4), far=(0, 1, 2, 3, 4, 7), direct=(1, 2, 3), sems=modes + 3,
+        scratch=(struct(2, width, width // 2), 1, 2, square),
     )
     powers = lax.all_to_all(power, "mode", 0, 0, tiled=True)
-    other = moved(own, "core", 1)
-    ahead, behind, extra = call(
-        outbound_kernel, "outbound", (own, other), [slot, slot, struct(8, width)], 1, copied=(0, 1)
-    )
-    from_behind = lax.ppermute(ahead, SCAN, [(i, (i + REACH) % scan_size) for i in range(scan_size)])
-    from_ahead = lax.ppermute(behind, SCAN, [(i, (i - REACH) % scan_size) for i in range(scan_size)])
+    places = range(scan_size)
+    edge = [(i, (i + 1) % scan_size if i % 2 else (i - 1) % scan_size) for i in places]
+    across = lax.ppermute(own, SCAN, edge)
+    next_chip = [(i, (i - 2) % scan_size if i % 2 else (i + 2) % scan_size) for i in places]
+    beyond = lax.ppermute(own, SCAN, next_chip)
+    combined, extra = call(partner_kernel, "partner", (own, across), [slot, struct(8, width)], 0)
+    partner = moved(combined, "core", 1)
     chunks, terms = call(
         main_kernel, "main",
-        (extra, powers, own, other, from_behind, from_ahead, turn, wave, tables, tile, own_probe),
+        (extra, powers, own, across, beyond, partner, turn, wave, tables, tile, own_probe),
         [struct(peers * CHUNK_ROWS, 128), plane_pair], 4,
-        copied=tuple(range(1, 11)), far=(6, 7, 8, 9, 10), direct=(0, 1), sems=1, scratch=(0, 1),
+        copied=tuple(range(6, 11)), far=(6, 7, 8, 9, 10), direct=(0,), sems=2, scratch=(0,),
     )
     arrived = lax.all_to_all(chunks.reshape(peers, 1, CHUNK_ROWS * 128), PLANE, 0, 0, tiled=True)
     others = [moved(terms, "mode", step) for step in (2, 1, 3)]
     [part] = call(plane_kernel, "plane", (arrived.reshape(peers * CHUNK_ROWS, 128),), [struct(24, 128)], 0)
     part_other = moved(part, "core", 1)
     spread, loss = call(
-        spread_kernel, "spread", (part, part_other), [struct(peers, 8, width), struct(8, 128)], 0
+        spread_kernel, "spread", (part, part_other), [struct(peers, 8, width), struct(8, 128)], 0,
+        direct=(0,), sems=7, scratch=(struct(peers // 8, 8, width),),
     )
     probe_total = lax.all_to_all(spread, PLANE, 0, 0, tiled=True)
     [object_total] = call(

time: 101 us -> 96.6 us (0.956)
  the two profiles are of different devices: /device:TPU:2 before, /device:TPU:1 now
where the time goes in v4:
time: 96.6 us; the launch traced here: 94.9 us
  starting transfers between devices  56.2 us (58%)
  waiting for transfers between devices  23.2 us (24%)
  Pallas kernels  10.3 us (11%)
  between operations  3.85 us (4%)
  local copies, waits for them, and re-layouts  1.31 us (1%)
    ppermute x5, starting transfers between devices, moved(): lax.ppermute(block, axis, [(i, (i + distance) % size) for i in range(size)])  23.1 us
    all_to_all x1, waiting for transfers between devices, body(): probe_total = lax.all_to_all(spread, PLANE, 0, 0, tiled=True)  14.9 us
    ppermute x1, starting transfers between devices, body(): beyond = lax.ppermute(own, SCAN, next_chip)  11.4 us
    pallas_call x6, Pallas kernels, call(): pl.pallas_call(kernel, out_shape=[pltpu.HBM(o.shape, o.dtype) if i in dir...  10.3 us
    all_to_all x1, starting transfers between devices, body(): lax.all_to_all(chunks.reshape(peers, 1, CHUNK_ROWS * 128), PLANE, 0, 0, t...  7.89 us
    all_to_all x1, waiting for transfers between devices, body(): lax.all_to_all(chunks.reshape(peers, 1, CHUNK_ROWS * 128), PLANE, 0, 0, t...  5.91 us
    all_to_all x1, starting transfers between devices, body(): probe_total = lax.all_to_all(spread, PLANE, 0, 0, tiled=True)  4.86 us
    all_to_all x1, starting transfers between devices, body(): powers = lax.all_to_all(power, 'mode', 0, 0, tiled=True)  4.85 us
  transfers between devices with their start and end apart: 10, of which 5 were waited for; matrix products, arithmetic and copies ran while one was open for 1% of the time, Pallas kernels for 2%

profile of v4, /device:TPU:1, one launch (start us, length us, event | category | flops | bytes accessed | tf_op | source)
XLA Modules:
  0.0 94.9 jit_solution(3347783888897183328)
XLA Ops:
  1.9 4.4 %forward.1 = (f32[264,256]{1,0:T(8,128)S(1)}, f32[2,256,256]{2,1,0:T(8,128)}, f32[2,256,256]{2,1,0:T(8,128)}, f32[4,256,256]{2,1,0:T(8,128)}) custom-call(f32[256,256]{1,0:T(8,128)} %phase_in.1, bf16[256,256]{1,0:T(8,128)(2,1)} %constant.9.clone.order_in, f32[2,256,256]{2,1,0:T(8,128)} %bitcast.9, f32[2,256,256]{2,1,0:T(8,128)} %bitcast.11, ...), custom_call_target="tpu_custom_call" | custom-call | flops 4400000000 | tf_op jit(solution)/shard_map/forward/pallas_call | solution.py:348
  6.3 4.9 %all-to-all-start = ((f32[4,256,256]{2,1,0:T(8,128)}), f32[4,256,256]{2,1,0:T(8,128)S(1)}, u32[]{:S(2)}, u32[]{:S(2)}) async-start(f32[4,256,256]{2,1,0:T(8,128)} %get-tuple-element.15), calls=%async_computation | async-start | bytes 2097152 | tf_op jit(solution)/shard_map/all_to_all | solution.py:377
  11.2 4.0 %collective-permute-start = (f32[264,256]{1,0:T(8,128)S(1)}, f32[264,256]{1,0:T(8,128)S(1)}, u32[]{:S(2)}, u32[]{:S(2)}) collective-permute-start(f32[264,256]{1,0:T(8,128)S(1)} %get-tuple-element.13.own), channel_id=1, source_target_pairs={{0,508},{4,8},{8,4},{12,16},{16,12},{20,24},{24,20},{28,32},{32,28... | collective-permute-start | bytes 811016 | tf_op jit(solution)/shard_map/ppermute | solution.py:380
  15.2 11.4 %collective-permute-start.1 = (f32[264,256]{1,0:T(8,128)S(1)}, f32[264,256]{1,0:T(8,128)S(1)}, u32[]{:S(2)}, u32[]{:S(2)}) collective-permute-start(f32[264,256]{1,0:T(8,128)S(1)} %get-tuple-element.13.own), channel_id=1, source_target_pairs={{0,8},{4,508},{8,16},{12,4},{16,24},{20,12},{24,32},{28,20},{32,40... | collective-permute-start | bytes 811016 | tf_op jit(solution)/shard_map/ppermute | solution.py:382
  26.7 0.0 collective-permute-done.across
  26.7 0.1 partner.1
  26.8 5.8 %collective-permute-start.2 = (f32[264,256]{1,0:T(8,128)S(1)}, f32[264,256]{1,0:T(8,128)S(1)}, u32[]{:S(2)}, u32[]{:S(2)}) collective-permute-start(f32[264,256]{1,0:T(8,128)S(1)} %get-tuple-element.16), channel_id=1, source_target_pairs={{0,4},{4,0},{1,5},{5,1},{2,6},{6,2},{3,7},{7,3},{8,12},{12,8},{9,1... | collective-permute-start | bytes 811016 | tf_op jit(solution)/shard_map/ppermute | solution.py:25
  32.6 0.0 collective-permute-done.1.beyond
  32.6 1.1 %collective-permute-done.2.partner = f32[264,256]{1,0:T(8,128)S(1)} collective-permute-done((f32[264,256]{1,0:T(8,128)S(1)}, f32[264,256]{1,0:T(8,128)S(1)}, u32[]{:S(2)}, u32[]{:S(2)}) %collective-permute-start.2) | collective-permute-done | bytes 270368 | tf_op jit(solution)/shard_map/ppermute | solution.py:25
  33.8 0.0 all-to-all-done.powers
  33.8 3.8 %main.1 = (f32[1088,128]{1,0:T(8,128)}, f32[2,256,256]{2,1,0:T(8,128)S(1)}) custom-call(f32[8,256]{1,0:T(8,128)S(1)} %get-tuple-element.14.extra, f32[4,256,256]{2,1,0:T(8,128)S(1)} %all-to-all-done.powers, f32[264,256]{1,0:T(8,128)S(1)} %get-tuple-element.13.own, f32[264,256]{1,0:T(8,128)S(1)} %collective-permute-done.across, ...), custom_call_target="tpu_custom_call" | custom-call | flops 4400000000 | tf_op jit(solution)/shard_map/main/pallas_call | solution.py:348
  37.6 7.9 %all-to-all-start.1 = ((f32[64,1,2176]{2,1,0:T(1,128)}), f32[64,1,2176]{2,1,0:T(1,128)S(1)}, u32[]{:S(2)}, u32[]{:S(2)}) async-start(f32[64,1,2176]{2,1,0:T(1,128)} %bitcast.8), calls=%async_computation.1 | async-start | bytes 1114112 | tf_op jit(solution)/shard_map/all_to_all | solution.py:391
  45.5 4.2 %collective-permute-start.5 = (f32[2,256,256]{2,1,0:T(8,128)S(1)}, f32[2,256,256]{2,1,0:T(8,128)S(1)}, u32[]{:S(2)}, u32[]{:S(2)}) collective-permute-start(f32[2,256,256]{2,1,0:T(8,128)S(1)} %get-tuple-element.19.own_in), channel_id=1, source_target_pairs={{0,3},{1,0},{2,1},{3,2},{4,7},{5,4},{6,5},{7,6},{8,11},{9,8},{10,9... | collective-permute-start | bytes 1572872 | tf_op jit(solution)/shard_map/ppermute | solution.py:25
  49.7 1.9 %collective-permute-start.4 = (f32[2,256,256]{2,1,0:T(8,128)S(1)}, f32[2,256,256]{2,1,0:T(8,128)S(1)}, u32[]{:S(2)}, u32[]{:S(2)}) collective-permute-start(f32[2,256,256]{2,1,0:T(8,128)S(1)} %get-tuple-element.19.own_in), channel_id=1, source_target_pairs={{0,1},{1,2},{2,3},{3,0},{4,5},{5,6},{6,7},{7,4},{8,9},{9,10},{10,1... | collective-permute-start | bytes 1572872 | tf_op jit(solution)/shard_map/ppermute | solution.py:25
  51.6 3.7 %collective-permute-start.3 = (f32[2,256,256]{2,1,0:T(8,128)S(1)}, f32[2,256,256]{2,1,0:T(8,128)S(1)}, u32[]{:S(2)}, u32[]{:S(2)}) collective-permute-start(f32[2,256,256]{2,1,0:T(8,128)S(1)} %get-tuple-element.19.own_in), channel_id=1, source_target_pairs={{0,2},{1,3},{2,0},{3,1},{4,6},{5,7},{6,4},{7,5},{8,10},{9,11},{10,... | collective-permute-start | bytes 1572872 | tf_op jit(solution)/shard_map/ppermute | solution.py:25
  55.3 5.9 %all-to-all-done.1 = f32[64,1,2176]{2,1,0:T(1,128)S(1)} async-done(((f32[64,1,2176]{2,1,0:T(1,128)}), f32[64,1,2176]{2,1,0:T(1,128)S(1)}, u32[]{:S(2)}, u32[]{:S(2)}) %all-to-all-start.1) | async-done | bytes 557088 | tf_op jit(solution)/shard_map/all_to_all | solution.py:391
  61.2 0.1 plane.1.one
  61.3 7.5 %collective-permute-start.6 = (f32[24,128]{1,0:T(8,128)S(1)}, f32[24,128]{1,0:T(8,128)S(1)}, u32[]{:S(2)}, u32[]{:S(2)}) collective-permute-start(f32[24,128]{1,0:T(8,128)S(1)} %plane.1.one), channel_id=1, source_target_pairs={{0,4},{4,0},{1,5},{5,1},{2,6},{6,2},{3,7},{7,3},{8,12},{12,8},{9,1... | collective-permute-start | bytes 36872 | tf_op jit(solution)/shard_map/ppermute | solution.py:25
  68.8 0.8 collective-permute-done.6.two
  69.6 0.9 spread.1
  70.5 4.9 %all-to-all-start.2 = ((f32[64,8,256]{2,1,0:T(8,128)}), f32[64,8,256]{2,1,0:T(8,128)S(1)}, u32[]{:S(2)}, u32[]{:S(2)}) async-start(f32[64,8,256]{2,1,0:T(8,128)} %get-tuple-element.21), calls=%async_computation.2 | async-start | bytes 1048576 | tf_op jit(solution)/shard_map/all_to_all | solution.py:399
  75.3 0.0 collective-permute-done.5.three_in
  75.3 0.0 collective-permute-done.4.two_in
  75.4 0.4 collective-permute-done.3.one_in
  75.8 1.1 %object.1 = f32[1,2,256,256]{3,2,1,0:T(8,128)} custom-call(f32[2,256,256]{2,1,0:T(8,128)S(1)} %get-tuple-element.19.own_in, f32[2,256,256]{2,1,0:T(8,128)S(1)} %collective-permute-done.3.one_in, f32[2,256,256]{2,1,0:T(8,128)S(1)} %collective-permute-done.4.two_in, f32[2,256,256]{2,1,0:T(8,128)S(1)} %collective-permute-done.5.three_in), custom_call_target="tpu_custom_call" | custom-call | flops 109999996928 | tf_op jit(solution)/shard_map/object/pallas_call | solution.py:348
  76.8 0.5 slice.3
  78.0 14.9 %all-to-all-done.2 = f32[64,8,256]{2,1,0:T(8,128)S(1)} async-done(((f32[64,8,256]{2,1,0:T(8,128)}), f32[64,8,256]{2,1,0:T(8,128)S(1)}, u32[]{:S(2)}, u32[]{:S(2)}) %all-to-all-start.2) | async-done | bytes 524320 | tf_op jit(solution)/shard_map/all_to_all | solution.py:399
  92.9 0.8 copy.15
Async XLA Ops:
  6.3 27.5 %all-to-all-start = ((f32[4,256,256]{2,1,0:T(8,128)}), f32[4,256,256]{2,1,0:T(8,128)S(1)}, u32[]{:S(2)}, u32[]{:S(2)}) async-start(f32[4,256,256]{2,1,0:T(8,128)} %get-tuple-element.15), calls=%async_computation | async-start | bytes 2097152 | tf_op jit(solution)/shard_map/all_to_all | solution.py:377
  11.2 15.5 %collective-permute-start = (f32[264,256]{1,0:T(8,128)S(1)}, f32[264,256]{1,0:T(8,128)S(1)}, u32[]{:S(2)}, u32[]{:S(2)}) collective-permute-start(f32[264,256]{1,0:T(8,128)S(1)} %get-tuple-element.13.own), channel_id=1, source_target_pairs={{0,508},{4,8},{8,4},{12,16},{16,12},{20,24},{24,20},{28,32},{32,28... | collective-permute-start | bytes 811016 | tf_op jit(solution)/shard_map/ppermute | solution.py:380
  15.2 17.4 %collective-permute-start.1 = (f32[264,256]{1,0:T(8,128)S(1)}, f32[264,256]{1,0:T(8,128)S(1)}, u32[]{:S(2)}, u32[]{:S(2)}) collective-permute-start(f32[264,256]{1,0:T(8,128)S(1)} %get-tuple-element.13.own), channel_id=1, source_target_pairs={{0,8},{4,508},{8,16},{12,4},{16,24},{20,12},{24,32},{28,20},{32,40... | collective-permute-start | bytes 811016 | tf_op jit(solution)/shard_map/ppermute | solution.py:382
  26.8 7.0 %collective-permute-start.2 = (f32[264,256]{1,0:T(8,128)S(1)}, f32[264,256]{1,0:T(8,128)S(1)}, u32[]{:S(2)}, u32[]{:S(2)}) collective-permute-start(f32[264,256]{1,0:T(8,128)S(1)} %get-tuple-element.16), channel_id=1, source_target_pairs={{0,4},{4,0},{1,5},{5,1},{2,6},{6,2},{3,7},{7,3},{8,12},{12,8},{9,1... | collective-permute-start | bytes 811016 | tf_op jit(solution)/shard_map/ppermute | solution.py:25
  37.6 23.6 %all-to-all-start.1 = ((f32[64,1,2176]{2,1,0:T(1,128)}), f32[64,1,2176]{2,1,0:T(1,128)S(1)}, u32[]{:S(2)}, u32[]{:S(2)}) async-start(f32[64,1,2176]{2,1,0:T(1,128)} %bitcast.8), calls=%async_computation.1 | async-start | bytes 1114112 | tf_op jit(solution)/shard_map/all_to_all | solution.py:391
  45.5 29.8 %collective-permute-start.5 = (f32[2,256,256]{2,1,0:T(8,128)S(1)}, f32[2,256,256]{2,1,0:T(8,128)S(1)}, u32[]{:S(2)}, u32[]{:S(2)}) collective-permute-start(f32[2,256,256]{2,1,0:T(8,128)S(1)} %get-tuple-element.19.own_in), channel_id=1, source_target_pairs={{0,3},{1,0},{2,1},{3,2},{4,7},{5,4},{6,5},{7,6},{8,11},{9,8},{10,9... | collective-permute-start | bytes 1572872 | tf_op jit(solution)/shard_map/ppermute | solution.py:25
  49.7 25.7 %collective-permute-start.4 = (f32[2,256,256]{2,1,0:T(8,128)S(1)}, f32[2,256,256]{2,1,0:T(8,128)S(1)}, u32[]{:S(2)}, u32[]{:S(2)}) collective-permute-start(f32[2,256,256]{2,1,0:T(8,128)S(1)} %get-tuple-element.19.own_in), channel_id=1, source_target_pairs={{0,1},{1,2},{2,3},{3,0},{4,5},{5,6},{6,7},{7,4},{8,9},{9,10},{10,1... | collective-permute-start | bytes 1572872 | tf_op jit(solution)/shard_map/ppermute | solution.py:25
  51.6 24.1 %collective-permute-start.3 = (f32[2,256,256]{2,1,0:T(8,128)S(1)}, f32[2,256,256]{2,1,0:T(8,128)S(1)}, u32[]{:S(2)}, u32[]{:S(2)}) collective-permute-start(f32[2,256,256]{2,1,0:T(8,128)S(1)} %get-tuple-element.19.own_in), channel_id=1, source_target_pairs={{0,2},{1,3},{2,0},{3,1},{4,6},{5,7},{6,4},{7,5},{8,10},{9,11},{10,... | collective-permute-start | bytes 1572872 | tf_op jit(solution)/shard_map/ppermute | solution.py:25
  61.3 8.3 %collective-permute-start.6 = (f32[24,128]{1,0:T(8,128)S(1)}, f32[24,128]{1,0:T(8,128)S(1)}, u32[]{:S(2)}, u32[]{:S(2)}) collective-permute-start(f32[24,128]{1,0:T(8,128)S(1)} %plane.1.one), channel_id=1, source_target_pairs={{0,4},{4,0},{1,5},{5,1},{2,6},{6,2},{3,7},{7,3},{8,12},{12,8},{9,1... | collective-permute-start | bytes 36872 | tf_op jit(solution)/shard_map/ppermute | solution.py:25
  70.5 22.5 %all-to-all-start.2 = ((f32[64,8,256]{2,1,0:T(8,128)}), f32[64,8,256]{2,1,0:T(8,128)S(1)}, u32[]{:S(2)}, u32[]{:S(2)}) async-start(f32[64,8,256]{2,1,0:T(8,128)} %get-tuple-element.21), calls=%async_computation.2 | async-start | bytes 1048576 | tf_op jit(solution)/shard_map/all_to_all | solution.py:399
